TPU v7x, 512 devices: a whole 4x8x8 slice. The times are simulated.
512 devices in a mesh: ty: 16 (over z, core), tx: 32 (over y, x).
Axes of the slice: x: 4, y: 8, z: 8, core: 2. Of those that a mesh axis runs over, the one named last changes fastest.
Arguments:
- excite_l0: float32 [16, 32, 1024], P(None, 'ty', 'tx'), may hold values from -6 to 6
- excite_l1: float32 [16, 64, 2048], P(None, 'ty', 'tx'), may hold values from -6 to 6
- excite_l2: float32 [16, 128, 4096], P(None, 'ty', 'tx'), may hold values from -6 to 6
- excite_l3: float32 [16, 256, 8192], P(None, 'ty', 'tx'), may hold values from -6 to 6
- refine_weights: float32 [3, 4, 9], replicated, may hold values from -2 to 2
- block_factor: float32 [3, 4, 4], replicated, may hold values from -3 to 3
- channel_factor: float32 [16, 16], replicated, may hold values from -1.5 to 1.5
- cotangent: float32 [16, 256, 8192], P(None, 'ty', 'tx'), may hold values from -6 to 6
Outputs:
- sky: float32 [16, 256, 8192], P(None, 'ty', 'tx')
- grad_l0: float32 [16, 32, 1024], P(None, 'ty', 'tx')
- grad_l1: float32 [16, 64, 2048], P(None, 'ty', 'tx')
- grad_l2: float32 [16, 128, 4096], P(None, 'ty', 'tx')
- grad_l3: float32 [16, 256, 8192], P(None, 'ty', 'tx')
All inputs are finite; a program needn't handle non-finite values.
Results may differ from a plain program's by a relative error of at most 0.00013.
Values sent between devices are 32-bit elements; how exact they have to be, the bound alone decides.
No kernel may reach another device: no remote copies, remote signals or barrier semaphores. Data moves between devices by JAX's collectives and lax.ppermute only.
A program may use at most 64 MiB of HBM per device.

v0:
```python
import jax
import jax.numpy as jnp
from jax import lax
from jax.sharding import PartitionSpec as P


def with_halo(block, sides, width):
    for axis, dim in sides:
        count = lax.axis_size(axis)
        forward = [(i, i + 1) for i in range(count - 1)]
        backward = [(target, source) for source, target in forward]
        low = lax.ppermute(
            lax.slice_in_dim(block, block.shape[dim] - width, None, axis=dim), axis, forward
        )
        high = lax.ppermute(lax.slice_in_dim(block, 0, width, axis=dim), axis, backward)
        block = jnp.concatenate([low, block, high], axis=dim)
    return block


def mix_channels(factor, field):
    return jnp.einsum("cd,dij->cij", factor, field, precision=lax.Precision.HIGHEST)


def mix_transposed(factor, field):
    return jnp.einsum("dc,dij->cij", factor, field, precision=lax.Precision.HIGHEST)


def to_blocks(field):
    chans, rows, cols = field.shape
    return (
        field.reshape(chans, rows // 2, 2, cols // 2, 2)
        .transpose(2, 4, 0, 1, 3)
        .reshape(4, chans, rows // 2, cols // 2)
    )


def from_blocks(blocks):
    chans, rows, cols = (blocks.shape[1], blocks.shape[2], blocks.shape[3])
    return (
        blocks.reshape(2, 2, chans, rows, cols)
        .transpose(2, 3, 0, 4, 1)
        .reshape(chans, 2 * rows, 2 * cols)
    )


def refine_level(padded, mixed, rmat, dmat):
    rows = padded.shape[1] - 2
    cols = padded.shape[2] - 2
    views = jnp.stack(
        [
            padded[:, 1 + da : 1 + da + rows, 1 + db : 1 + db + cols]
            for da in (-1, 0, 1)
            for db in (-1, 0, 1)
        ]
    )
    finer = jnp.einsum("kn,ncij->kcij", rmat, views, precision=lax.Precision.HIGHEST)
    finer = finer + jnp.einsum(
        "km,mcij->kcij", dmat, to_blocks(mixed), precision=lax.Precision.HIGHEST
    )
    return from_blocks(finer)


def pull_coarse(upward, rmat, rows, cols):
    spread = jnp.einsum("kn,kcij->ncij", rmat, to_blocks(upward), precision=lax.Precision.HIGHEST)
    coarse = jnp.zeros((upward.shape[0], rows, cols), jnp.float32)
    for da in (-1, 0, 1):
        for db in (-1, 0, 1):
            index = 3 * (da + 1) + db + 1
            coarse = coarse + spread[index, :, 1 - da : 1 - da + rows, 1 - db : 1 - db + cols]
    return coarse


def on_device(
    excite_l0,
    excite_l1,
    excite_l2,
    excite_l3,
    refine_weights,
    block_factor,
    channel_factor,
    cotangent,
):
    excites = [excite_l0, excite_l1, excite_l2, excite_l3]
    field = mix_channels(channel_factor, excite_l0)
    for level in range(1, 4):
        padded = with_halo(field, (("ty", 1), ("tx", 2)), 1)
        field = refine_level(
            padded,
            mix_channels(channel_factor, excites[level]),
            refine_weights[level - 1],
            block_factor[level - 1],
        )
    grads = [None, None, None, None]
    upward = cotangent
    for level in (3, 2, 1):
        rmat = refine_weights[level - 1]
        dmat = block_factor[level - 1]
        along = jnp.einsum(
            "km,kcij->mcij", dmat, to_blocks(upward), precision=lax.Precision.HIGHEST
        )
        grads[level] = mix_transposed(channel_factor, from_blocks(along))
        widened_grad = with_halo(upward, (("ty", 1), ("tx", 2)), 2)
        upward = pull_coarse(widened_grad, rmat, upward.shape[1] // 2, upward.shape[2] // 2)
    grads[0] = mix_transposed(channel_factor, upward)
    return (field, grads[0], grads[1], grads[2], grads[3])


def solution(mesh):
    placed = (
        P(None, "ty", "tx"),
        P(None, "ty", "tx"),
        P(None, "ty", "tx"),
        P(None, "ty", "tx"),
        P(),
        P(),
        P(),
        P(None, "ty", "tx"),
    )
    return jax.shard_map(
        on_device,
        mesh=mesh,
        in_specs=placed,
        out_specs=(
            P(None, "ty", "tx"),
            P(None, "ty", "tx"),
            P(None, "ty", "tx"),
            P(None, "ty", "tx"),
            P(None, "ty", "tx"),
        ),
        check_vma=False,
    )
```

profile of v0, /device:TPU:223, one launch (start us, length us, event | category | flops | bytes accessed | tf_op | source)
XLA Modules:
  0.0 180.0 jit_solution(2113394910568545431)
XLA Ops:
  0.7 1.7 fusion.55
  2.3 5.8 %collective-permute-start.12 = (f32[16,2,256]{2,1,0:T(2,128)}, f32[16,2,256]{2,1,0:T(2,128)}, u32[]{:S(2)}, u32[]{:S(2)}) collective-permute-start(f32[16,2,256]{2,1,0:T(2,128)} %get-tuple-element.22), channel_id=1, source_target_pairs={{0,32},{32,64},{64,96},{96,128},{128,160},{160,192},{192,224},{224... | collective-permute-start | bytes 98312 | tf_op jit(solution)/shard_map/ppermute | solution.py:12
  8.1 1.9 %collective-permute-start.13 = (f32[16,2,256]{2,1,0:T(2,128)}, f32[16,2,256]{2,1,0:T(2,128)}, u32[]{:S(2)}, u32[]{:S(2)}) collective-permute-start(f32[16,2,256]{2,1,0:T(2,128)} %get-tuple-element.23), channel_id=1, source_target_pairs={{32,0},{64,32},{96,64},{128,96},{160,128},{192,160},{224,192},{256... | collective-permute-start | bytes 98312 | tf_op jit(solution)/shard_map/ppermute | solution.py:15
  10.9 4.9 %collective-permute-start = (f32[16,1,32]{2,0,1:T(8,128)S(1)}, f32[16,1,32]{2,0,1:T(8,128)S(1)}, u32[]{:S(2)}, u32[]{:S(2)}) collective-permute-start(f32[16,1,32]{2,0,1:T(8,128)S(1)} %get-tuple-element.62), channel_id=1, source_target_pairs={{0,32},{32,64},{64,96},{96,128},{128,160},{160,192},{192,224},{224... | collective-permute-start | bytes 6152 | tf_op jit(solution)/shard_map/ppermute | solution.py:12
  15.8 1.9 %collective-permute-start.1 = (f32[16,1,32]{2,0,1:T(8,128)S(1)}, f32[16,1,32]{2,0,1:T(8,128)S(1)}, u32[]{:S(2)}, u32[]{:S(2)}) collective-permute-start(f32[16,1,32]{2,0,1:T(8,128)S(1)} %get-tuple-element.63), channel_id=1, source_target_pairs={{32,0},{64,32},{96,64},{128,96},{160,128},{192,160},{224,192},{256... | collective-permute-start | bytes 6152 | tf_op jit(solution)/shard_map/ppermute | solution.py:15
  17.7 2.9 %copy.183 = f32[16,16,256]{0,2,1:T(8,128)} copy(f32[16,16,256]{2,1,0:T(8,128)} %param.15) | data formatting | bytes 524288 | tf_op args[7]
  21.6 3.4 %fusion.4 = f32[16,16,256]{0,2,1:T(8,128)S(1)} fusion(f32[16,16,256]{2,1,0:T(8,128)S(1)} %copy-done, f32[16,16]{1,0:T(8,128)S(1)} %copy-done.2), kind=kOutput, calls=%fused_computation.18 | convolution fusion | flops 12582912 | bytes 525312 | tf_op jit(solution)/shard_map/cd,dij->cij/dot_general | solution.py:21
  25.1 1.9 %copy.184 = f32[2,2,16,8,128]{4,3,2,1,0:T(8,128)S(1)} copy(f32[2,2,16,8,128]{2,1,4,0,3:T(2,128)} %bitcast.261) | data formatting | bytes 524288 | tf_op jit(solution)/shard_map/transpose | solution.py:32
  29.8 4.3 %collective-permute-start.2 = (f32[16,4,1]{2,0,1:T(8,128)}, f32[16,4,1]{2,0,1:T(8,128)S(1)}, u32[]{:S(2)}, u32[]{:S(2)}) collective-permute-start(f32[16,4,1]{2,0,1:T(8,128)} %get-tuple-element.61), channel_id=1, source_target_pairs={{0,1},{1,2},{2,3},{3,4},{4,5},{5,6},{6,7},{7,8},{8,9},{9,10},{10,1... | collective-permute-start | bytes 776 | tf_op jit(solution)/shard_map/ppermute | solution.py:12
  34.1 1.9 %collective-permute-start.3 = (f32[16,4,1]{2,0,1:T(8,128)}, f32[16,4,1]{2,0,1:T(8,128)}, u32[]{:S(2)}, u32[]{:S(2)}) collective-permute-start(f32[16,4,1]{2,0,1:T(8,128)} %get-tuple-element.60), channel_id=1, source_target_pairs={{1,0},{2,1},{3,2},{4,3},{5,4},{6,5},{7,6},{8,7},{9,8},{10,9},{11,1... | collective-permute-start | bytes 776 | tf_op jit(solution)/shard_map/ppermute | solution.py:15
  37.0 5.4 %collective-permute-done.3 = f32[16,4,1]{2,0,1:T(8,128)} collective-permute-done((f32[16,4,1]{2,0,1:T(8,128)}, f32[16,4,1]{2,0,1:T(8,128)}, u32[]{:S(2)}, u32[]{:S(2)}) %collective-permute-start.3) | collective-permute-done | bytes 288 | tf_op jit(solution)/shard_map/ppermute | solution.py:15
  45.0 1.1 fusion.6
  47.3 6.3 %collective-permute-start.4 = (f32[16,1,64]{2,1,0:T(1,128)S(1)}, f32[16,1,64]{2,1,0:T(1,128)S(1)}, u32[]{:S(2)}, u32[]{:S(2)}) collective-permute-start(f32[16,1,64]{2,1,0:T(1,128)S(1)} %get-tuple-element.56), channel_id=1, source_target_pairs={{0,32},{32,64},{64,96},{96,128},{128,160},{160,192},{192,224},{224... | collective-permute-start | bytes 12296 | tf_op jit(solution)/shard_map/ppermute | solution.py:12
  53.5 1.9 %collective-permute-start.5 = (f32[16,1,64]{2,1,0:T(1,128)S(1)}, f32[16,1,64]{2,1,0:T(1,128)S(1)}, u32[]{:S(2)}, u32[]{:S(2)}) collective-permute-start(f32[16,1,64]{2,1,0:T(1,128)S(1)} %get-tuple-element.57), channel_id=1, source_target_pairs={{32,0},{64,32},{96,64},{128,96},{160,128},{192,160},{224,192},{256... | collective-permute-start | bytes 12296 | tf_op jit(solution)/shard_map/ppermute | solution.py:15
  55.5 1.1 fusion.10
  56.6 2.3 %copy.186 = f32[16,8,2,128,2]{0,4,3,2,1:T(2,128)} copy(f32[16,8,2,128,2]{3,4,1,0,2:T(2,128)S(1)} %convolution_bitcast_fusion.3) | data formatting | bytes 524288 | tf_op jit(solution)/shard_map/transpose | solution.py:41
  59.8 1.9 %collective-permute-start.6 = (f32[16,6,1]{2,1,0:T(8,128)S(1)}, f32[16,6,1]{2,1,0:T(8,128)S(1)}, u32[]{:S(2)}, u32[]{:S(2)}) collective-permute-start(f32[16,6,1]{2,1,0:T(8,128)S(1)} %get-tuple-element.49), channel_id=1, source_target_pairs={{0,1},{1,2},{2,3},{3,4},{4,5},{5,6},{6,7},{7,8},{8,9},{9,10},{10,1... | collective-permute-start | bytes 1160 | tf_op jit(solution)/shard_map/ppermute | solution.py:12
  61.8 3.4 %collective-permute-start.7 = (f32[16,6,1]{2,1,0:T(8,128)S(1)}, f32[16,6,1]{2,1,0:T(8,128)S(1)}, u32[]{:S(2)}, u32[]{:S(2)}) collective-permute-start(f32[16,6,1]{2,1,0:T(8,128)S(1)} %get-tuple-element.48), channel_id=1, source_target_pairs={{1,0},{2,1},{3,2},{4,3},{5,4},{6,5},{7,6},{8,7},{9,8},{10,9},{11,1... | collective-permute-start | bytes 1160 | tf_op jit(solution)/shard_map/ppermute | solution.py:15
  65.2 4.9 %collective-permute-done.7 = f32[16,6,1]{2,1,0:T(8,128)S(1)} collective-permute-done((f32[16,6,1]{2,1,0:T(8,128)S(1)}, f32[16,6,1]{2,1,0:T(8,128)S(1)}, u32[]{:S(2)}, u32[]{:S(2)}) %collective-permute-start.7) | collective-permute-done | bytes 416 | tf_op jit(solution)/shard_map/ppermute | solution.py:15
  71.7 5.3 %collective-permute-start.8 = (f32[16,1,128]{2,1,0:T(1,128)S(1)}, f32[16,1,128]{2,1,0:T(1,128)S(1)}, u32[]{:S(2)}, u32[]{:S(2)}) collective-permute-start(f32[16,1,128]{2,1,0:T(1,128)S(1)} %get-tuple-element.40), channel_id=1, source_target_pairs={{0,32},{32,64},{64,96},{96,128},{128,160},{160,192},{192,224},{224... | collective-permute-start | bytes 24584 | tf_op jit(solution)/shard_map/ppermute | solution.py:12
  77.0 2.1 %collective-permute-start.9 = (f32[16,1,128]{2,1,0:T(1,128)S(1)}, f32[16,1,128]{2,1,0:T(1,128)S(1)}, u32[]{:S(2)}, u32[]{:S(2)}) collective-permute-start(f32[16,1,128]{2,1,0:T(1,128)S(1)} %get-tuple-element.41), channel_id=1, source_target_pairs={{32,0},{64,32},{96,64},{128,96},{160,128},{192,160},{224,192},{256... | collective-permute-start | bytes 24584 | tf_op jit(solution)/shard_map/ppermute | solution.py:15
  79.1 3.5 %convolution_bitcast_fusion.4 = f32[16,16,256]{2,0,1:T(8,128)S(1)} fusion(f32[16,16,256]{0,2,1:T(8,128)} %bitcast.260, f32[16,16]{1,0:T(8,128)S(1)} %copy-done.3), kind=kOutput, calls=%fused_computation.5 | convolution fusion | flops 12582912 | bytes 525312 | tf_op jit(solution)/shard_map/dc,dij->cij/dot_general | solution.py:25
  83.6 1.9 %collective-permute-start.11 = (f32[16,10,1]{2,1,0:T(8,128)S(1)}, f32[16,10,1]{2,1,0:T(8,128)S(1)}, u32[]{:S(2)}, u32[]{:S(2)}) collective-permute-start(f32[16,10,1]{2,1,0:T(8,128)S(1)} %get-tuple-element.32), channel_id=1, source_target_pairs={{1,0},{2,1},{3,2},{4,3},{5,4},{6,5},{7,6},{8,7},{9,8},{10,9},{11,1... | collective-permute-start | bytes 1928 | tf_op jit(solution)/shard_map/ppermute | solution.py:15
  85.5 1.4 fusion.2
  88.0 6.7 %collective-permute-start.10 = (f32[16,10,1]{2,1,0:T(8,128)S(1)}, f32[16,10,1]{2,1,0:T(8,128)S(1)}, u32[]{:S(2)}, u32[]{:S(2)}) collective-permute-start(f32[16,10,1]{2,1,0:T(8,128)S(1)} %get-tuple-element.33), channel_id=1, source_target_pairs={{0,1},{1,2},{2,3},{3,4},{4,5},{5,6},{6,7},{7,8},{8,9},{9,10},{10,1... | collective-permute-start | bytes 1928 | tf_op jit(solution)/shard_map/ppermute | solution.py:12
  94.9 1.7 collective-permute-done.10
  98.8 7.1 %collective-permute-start.14 = (f32[16,20,2]{2,1,0:T(8,128)S(1)}, f32[16,20,2]{2,1,0:T(8,128)S(1)}, u32[]{:S(2)}, u32[]{:S(2)}) collective-permute-start(f32[16,20,2]{2,1,0:T(8,128)S(1)} %get-tuple-element.20), channel_id=1, source_target_pairs={{0,1},{1,2},{2,3},{3,4},{4,5},{5,6},{6,7},{7,8},{8,9},{9,10},{10,1... | collective-permute-start | bytes 7688 | tf_op jit(solution)/shard_map/ppermute | solution.py:12
  105.9 1.9 %collective-permute-start.15 = (f32[16,20,2]{2,1,0:T(8,128)S(1)}, f32[16,20,2]{2,1,0:T(8,128)}, u32[]{:S(2)}, u32[]{:S(2)}) collective-permute-start(f32[16,20,2]{2,1,0:T(8,128)S(1)} %get-tuple-element.21), channel_id=1, source_target_pairs={{1,0},{2,1},{3,2},{4,3},{5,4},{6,5},{7,6},{8,7},{9,8},{10,9},{11,1... | collective-permute-start | bytes 7688 | tf_op jit(solution)/shard_map/ppermute | solution.py:15
  108.5 1.1 copy.159
  109.7 1.3 copy.189
  111.7 5.4 %collective-permute-done.15 = f32[16,20,2]{2,1,0:T(8,128)} collective-permute-done((f32[16,20,2]{2,1,0:T(8,128)S(1)}, f32[16,20,2]{2,1,0:T(8,128)}, u32[]{:S(2)}, u32[]{:S(2)}) %collective-permute-start.15) | collective-permute-done | bytes 2592 | tf_op jit(solution)/shard_map/ppermute | solution.py:15
  117.1 1.4 pad_maximum_fusion
  118.6 1.7 copy.160
  120.3 2.7 %reshape.145 = f32[16,10,2,130,2]{0,4,3,2,1:T(2,128)} reshape(f32[16,20,260]{0,2,1:T(8,128)S(1)} %copy.160) | data formatting | bytes 665600 | tf_op jit(solution)/shard_map/reshape | solution.py:31
  123.0 4.2 %copy.161 = f32[2,2,16,10,130]{4,1,0,3,2:T(2,128)S(1)} copy(f32[2,2,16,10,130]{2,1,4,0,3:T(2,128)} %bitcast.258) | data formatting | bytes 665600 | tf_op jit(solution)/shard_map/transpose | solution.py:32
  127.8 2.2 %convolution_bitcast_fusion = f32[9,16,10,130]{3,0,2,1:T(8,128)S(1)} fusion(f32[4,16,10,130]{3,0,2,1:T(4,128)S(1)} %reshape.146, f32[3,4,9]{2,1,0:T(4,128)S(1)} %copy-done.13), kind=kOutput, calls=%fused_computation | convolution fusion | flops 8985600 | bytes 1406208 | tf_op jit(solution)/shard_map/kn,kcij->ncij/dot_general | solution.py:64
  131.1 6.3 %collective-permute-start.16 = (f32[16,2,128]{2,1,0:T(2,128)S(1)}, f32[16,2,128]{2,1,0:T(2,128)S(1)}, u32[]{:S(2)}, u32[]{:S(2)}) collective-permute-start(f32[16,2,128]{2,1,0:T(2,128)S(1)} %get-tuple-element.38), channel_id=1, source_target_pairs={{0,32},{32,64},{64,96},{96,128},{128,160},{160,192},{192,224},{224... | collective-permute-start | bytes 49160 | tf_op jit(solution)/shard_map/ppermute | solution.py:12
  137.4 2.1 %collective-permute-start.17 = (f32[16,2,128]{2,1,0:T(2,128)S(1)}, f32[16,2,128]{2,1,0:T(2,128)S(1)}, u32[]{:S(2)}, u32[]{:S(2)}) collective-permute-start(f32[16,2,128]{2,1,0:T(2,128)S(1)} %get-tuple-element.39), channel_id=1, source_target_pairs={{32,0},{64,32},{96,64},{128,96},{160,128},{192,160},{224,192},{256... | collective-permute-start | bytes 49160 | tf_op jit(solution)/shard_map/ppermute | solution.py:15
  140.5 3.2 %collective-permute-done.17 = f32[16,2,128]{2,1,0:T(2,128)S(1)} collective-permute-done((f32[16,2,128]{2,1,0:T(2,128)S(1)}, f32[16,2,128]{2,1,0:T(2,128)S(1)}, u32[]{:S(2)}, u32[]{:S(2)}) %collective-permute-start.17) | collective-permute-done | bytes 16416 | tf_op jit(solution)/shard_map/ppermute | solution.py:15
  143.8 1.9 %collective-permute-start.18 = (f32[16,12,2]{2,1,0:T(8,128)S(1)}, f32[16,12,2]{2,1,0:T(8,128)S(1)}, u32[]{:S(2)}, u32[]{:S(2)}) collective-permute-start(f32[16,12,2]{2,1,0:T(8,128)S(1)} %get-tuple-element.30), channel_id=1, source_target_pairs={{0,1},{1,2},{2,3},{3,4},{4,5},{5,6},{6,7},{7,8},{8,9},{9,10},{10,1... | collective-permute-start | bytes 4616 | tf_op jit(solution)/shard_map/ppermute | solution.py:12
  145.8 3.4 %collective-permute-start.19 = (f32[16,12,2]{2,1,0:T(8,128)S(1)}, f32[16,12,2]{2,1,0:T(8,128)S(1)}, u32[]{:S(2)}, u32[]{:S(2)}) collective-permute-start(f32[16,12,2]{2,1,0:T(8,128)S(1)} %get-tuple-element.31), channel_id=1, source_target_pairs={{1,0},{2,1},{3,2},{4,3},{5,4},{6,5},{7,6},{8,7},{9,8},{10,9},{11,1... | collective-permute-start | bytes 4616 | tf_op jit(solution)/shard_map/ppermute | solution.py:15
  150.4 4.4 %collective-permute-done.19 = f32[16,12,2]{2,1,0:T(8,128)S(1)} collective-permute-done((f32[16,12,2]{2,1,0:T(8,128)S(1)}, f32[16,12,2]{2,1,0:T(8,128)S(1)}, u32[]{:S(2)}, u32[]{:S(2)}) %collective-permute-start.19) | collective-permute-done | bytes 1568 | tf_op jit(solution)/shard_map/ppermute | solution.py:15
  157.8 3.2 %collective-permute-start.20 = (f32[16,2,64]{2,1,0:T(2,128)S(1)}, f32[16,2,64]{2,1,0:T(2,128)S(1)}, u32[]{:S(2)}, u32[]{:S(2)}) collective-permute-start(f32[16,2,64]{2,1,0:T(2,128)S(1)} %get-tuple-element.52), channel_id=1, source_target_pairs={{0,32},{32,64},{64,96},{96,128},{128,160},{160,192},{192,224},{224... | collective-permute-start | bytes 24584 | tf_op jit(solution)/shard_map/ppermute | solution.py:12
  161.0 1.9 %collective-permute-start.21 = (f32[16,2,64]{2,1,0:T(2,128)S(1)}, f32[16,2,64]{2,1,0:T(2,128)S(1)}, u32[]{:S(2)}, u32[]{:S(2)}) collective-permute-start(f32[16,2,64]{2,1,0:T(2,128)S(1)} %get-tuple-element.53), channel_id=1, source_target_pairs={{32,0},{64,32},{96,64},{128,96},{160,128},{192,160},{224,192},{256... | collective-permute-start | bytes 24584 | tf_op jit(solution)/shard_map/ppermute | solution.py:15
  163.5 3.8 %collective-permute-done.21 = f32[16,2,64]{2,1,0:T(2,128)S(1)} collective-permute-done((f32[16,2,64]{2,1,0:T(2,128)S(1)}, f32[16,2,64]{2,1,0:T(2,128)S(1)}, u32[]{:S(2)}, u32[]{:S(2)}) %collective-permute-start.21) | collective-permute-done | bytes 8224 | tf_op jit(solution)/shard_map/ppermute | solution.py:15
  167.4 1.9 %collective-permute-start.22 = (f32[16,8,2]{2,1,0:T(8,128)S(1)}, f32[16,8,2]{2,1,0:T(8,128)S(1)}, u32[]{:S(2)}, u32[]{:S(2)}) collective-permute-start(f32[16,8,2]{2,1,0:T(8,128)S(1)} %get-tuple-element.36), channel_id=1, source_target_pairs={{0,1},{1,2},{2,3},{3,4},{4,5},{5,6},{6,7},{7,8},{8,9},{9,10},{10,1... | collective-permute-start | bytes 3080 | tf_op jit(solution)/shard_map/ppermute | solution.py:12
  169.3 3.4 %collective-permute-start.23 = (f32[16,8,2]{2,1,0:T(8,128)S(1)}, f32[16,8,2]{2,1,0:T(8,128)S(1)}, u32[]{:S(2)}, u32[]{:S(2)}) collective-permute-start(f32[16,8,2]{2,1,0:T(8,128)S(1)} %get-tuple-element.37), channel_id=1, source_target_pairs={{1,0},{2,1},{3,2},{4,3},{5,4},{6,5},{7,6},{8,7},{9,8},{10,9},{11,1... | collective-permute-start | bytes 3080 | tf_op jit(solution)/shard_map/ppermute | solution.py:15
  173.8 3.9 %collective-permute-done.23 = f32[16,8,2]{2,1,0:T(8,128)S(1)} collective-permute-done((f32[16,8,2]{2,1,0:T(8,128)S(1)}, f32[16,8,2]{2,1,0:T(8,128)S(1)}, u32[]{:S(2)}, u32[]{:S(2)}) %collective-permute-start.23) | collective-permute-done | bytes 1056 | tf_op jit(solution)/shard_map/ppermute | solution.py:15
  (124 shorter events, 28.4 us)
Async XLA Ops:
  0.6 21.0 %copy-start = (f32[16,16,256]{2,1,0:T(8,128)S(1)}, f32[16,16,256]{2,1,0:T(8,128)}, u32[]{:S(2)}) copy-start(f32[16,16,256]{2,1,0:T(8,128)} %param.11) | copy-start | bytes 786436
  0.6 20.0 %copy-start.2 = (f32[16,16]{1,0:T(8,128)S(1)}, f32[16,16]{1,0:T(8,128)}, u32[]{:S(2)}) copy-start(f32[16,16]{1,0:T(8,128)} %param.14) | copy-start | bytes 3076
  0.7 20.0 %copy-start.8 = (f32[16,8,128]{2,1,0:T(8,128)S(1)}, f32[16,8,128]{2,1,0:T(8,128)}, u32[]{:S(2)}) copy-start(f32[16,8,128]{2,1,0:T(8,128)} %param.10) | copy-start | bytes 196612
  2.3 95.4 %collective-permute-start.12 = (f32[16,2,256]{2,1,0:T(2,128)}, f32[16,2,256]{2,1,0:T(2,128)}, u32[]{:S(2)}, u32[]{:S(2)}) collective-permute-start(f32[16,2,256]{2,1,0:T(2,128)} %get-tuple-element.22), channel_id=1, source_target_pairs={{0,32},{32,64},{64,96},{96,128},{128,160},{160,192},{192,224},{224... | collective-permute-start | bytes 98312 | tf_op jit(solution)/shard_map/ppermute | solution.py:12
  8.1 89.7 %collective-permute-start.13 = (f32[16,2,256]{2,1,0:T(2,128)}, f32[16,2,256]{2,1,0:T(2,128)}, u32[]{:S(2)}, u32[]{:S(2)}) collective-permute-start(f32[16,2,256]{2,1,0:T(2,128)} %get-tuple-element.23), channel_id=1, source_target_pairs={{32,0},{64,32},{96,64},{128,96},{160,128},{192,160},{224,192},{256... | collective-permute-start | bytes 98312 | tf_op jit(solution)/shard_map/ppermute | solution.py:15
  10.9 18.1 %collective-permute-start = (f32[16,1,32]{2,0,1:T(8,128)S(1)}, f32[16,1,32]{2,0,1:T(8,128)S(1)}, u32[]{:S(2)}, u32[]{:S(2)}) collective-permute-start(f32[16,1,32]{2,0,1:T(8,128)S(1)} %get-tuple-element.62), channel_id=1, source_target_pairs={{0,32},{32,64},{64,96},{96,128},{128,160},{160,192},{192,224},{224... | collective-permute-start | bytes 6152 | tf_op jit(solution)/shard_map/ppermute | solution.py:12
  15.8 13.3 %collective-permute-start.1 = (f32[16,1,32]{2,0,1:T(8,128)S(1)}, f32[16,1,32]{2,0,1:T(8,128)S(1)}, u32[]{:S(2)}, u32[]{:S(2)}) collective-permute-start(f32[16,1,32]{2,0,1:T(8,128)S(1)} %get-tuple-element.63), channel_id=1, source_target_pairs={{32,0},{64,32},{96,64},{128,96},{160,128},{192,160},{224,192},{256... | collective-permute-start | bytes 6152 | tf_op jit(solution)/shard_map/ppermute | solution.py:15
  21.6 7.0 %copy-start.10 = (f32[16,4,64]{2,1,0:T(4,128)S(1)}, f32[16,4,64]{2,1,0:T(4,128)}, u32[]{:S(2)}) copy-start(f32[16,4,64]{2,1,0:T(4,128)} %param.9) | copy-start | bytes 49156
  29.0 7.1 %copy-start.7 = (f32[16,1,32]{2,0,1:T(8,128)}, f32[16,1,32]{2,0,1:T(8,128)S(1)}, u32[]{:S(2)}) copy-start(f32[16,1,32]{2,0,1:T(8,128)S(1)} %collective-permute-done) | copy-start | bytes 6148
  29.1 7.1 %copy-start.6 = (f32[16,1,32]{2,0,1:T(8,128)}, f32[16,1,32]{2,0,1:T(8,128)S(1)}, u32[]{:S(2)}) copy-start(f32[16,1,32]{2,0,1:T(8,128)S(1)} %collective-permute-done.1) | copy-start | bytes 6148
  29.8 6.6 %collective-permute-start.2 = (f32[16,4,1]{2,0,1:T(8,128)}, f32[16,4,1]{2,0,1:T(8,128)S(1)}, u32[]{:S(2)}, u32[]{:S(2)}) collective-permute-start(f32[16,4,1]{2,0,1:T(8,128)} %get-tuple-element.61), channel_id=1, source_target_pairs={{0,1},{1,2},{2,3},{3,4},{4,5},{5,6},{6,7},{7,8},{8,9},{9,10},{10,1... | collective-permute-start | bytes 776 | tf_op jit(solution)/shard_map/ppermute | solution.py:12
  34.1 8.3 %collective-permute-start.3 = (f32[16,4,1]{2,0,1:T(8,128)}, f32[16,4,1]{2,0,1:T(8,128)}, u32[]{:S(2)}, u32[]{:S(2)}) collective-permute-start(f32[16,4,1]{2,0,1:T(8,128)} %get-tuple-element.60), channel_id=1, source_target_pairs={{1,0},{2,1},{3,2},{4,3},{5,4},{6,5},{7,6},{8,7},{9,8},{10,9},{11,1... | collective-permute-start | bytes 776 | tf_op jit(solution)/shard_map/ppermute | solution.py:15
  36.3 0.6 copy-start.9
  47.3 11.7 %collective-permute-start.4 = (f32[16,1,64]{2,1,0:T(1,128)S(1)}, f32[16,1,64]{2,1,0:T(1,128)S(1)}, u32[]{:S(2)}, u32[]{:S(2)}) collective-permute-start(f32[16,1,64]{2,1,0:T(1,128)S(1)} %get-tuple-element.56), channel_id=1, source_target_pairs={{0,32},{32,64},{64,96},{96,128},{128,160},{160,192},{192,224},{224... | collective-permute-start | bytes 12296 | tf_op jit(solution)/shard_map/ppermute | solution.py:12
  53.5 6.2 %collective-permute-start.5 = (f32[16,1,64]{2,1,0:T(1,128)S(1)}, f32[16,1,64]{2,1,0:T(1,128)S(1)}, u32[]{:S(2)}, u32[]{:S(2)}) collective-permute-start(f32[16,1,64]{2,1,0:T(1,128)S(1)} %get-tuple-element.57), channel_id=1, source_target_pairs={{32,0},{64,32},{96,64},{128,96},{160,128},{192,160},{224,192},{256... | collective-permute-start | bytes 12296 | tf_op jit(solution)/shard_map/ppermute | solution.py:15
  56.6 14.2 %copy-start.12 = (f32[3,4,9]{2,1,0:T(4,128)S(1)}, f32[3,4,9]{2,1,0:T(4,128)}, u32[]{:S(2)}) copy-start(f32[3,4,9]{2,1,0:T(4,128)} %param.12) | copy-start | bytes 1300
  58.9 20.2 %copy-start.3 = (f32[16,16]{1,0:T(8,128)S(1)}, f32[16,16]{1,0:T(8,128)}, u32[]{:S(2)}) copy-start(f32[16,16]{1,0:T(8,128)} %param.14) | copy-start | bytes 3076
  59.8 5.3 %collective-permute-start.6 = (f32[16,6,1]{2,1,0:T(8,128)S(1)}, f32[16,6,1]{2,1,0:T(8,128)S(1)}, u32[]{:S(2)}, u32[]{:S(2)}) collective-permute-start(f32[16,6,1]{2,1,0:T(8,128)S(1)} %get-tuple-element.49), channel_id=1, source_target_pairs={{0,1},{1,2},{2,3},{3,4},{4,5},{5,6},{6,7},{7,8},{8,9},{9,10},{10,1... | collective-permute-start | bytes 1160 | tf_op jit(solution)/shard_map/ppermute | solution.py:12
  61.8 8.3 %collective-permute-start.7 = (f32[16,6,1]{2,1,0:T(8,128)S(1)}, f32[16,6,1]{2,1,0:T(8,128)S(1)}, u32[]{:S(2)}, u32[]{:S(2)}) collective-permute-start(f32[16,6,1]{2,1,0:T(8,128)S(1)} %get-tuple-element.48), channel_id=1, source_target_pairs={{1,0},{2,1},{3,2},{4,3},{5,4},{6,5},{7,6},{8,7},{9,8},{10,9},{11,1... | collective-permute-start | bytes 1160 | tf_op jit(solution)/shard_map/ppermute | solution.py:15
  71.7 11.7 %collective-permute-start.8 = (f32[16,1,128]{2,1,0:T(1,128)S(1)}, f32[16,1,128]{2,1,0:T(1,128)S(1)}, u32[]{:S(2)}, u32[]{:S(2)}) collective-permute-start(f32[16,1,128]{2,1,0:T(1,128)S(1)} %get-tuple-element.40), channel_id=1, source_target_pairs={{0,32},{32,64},{64,96},{96,128},{128,160},{160,192},{192,224},{224... | collective-permute-start | bytes 24584 | tf_op jit(solution)/shard_map/ppermute | solution.py:12
  77.0 6.4 %collective-permute-start.9 = (f32[16,1,128]{2,1,0:T(1,128)S(1)}, f32[16,1,128]{2,1,0:T(1,128)S(1)}, u32[]{:S(2)}, u32[]{:S(2)}) collective-permute-start(f32[16,1,128]{2,1,0:T(1,128)S(1)} %get-tuple-element.41), channel_id=1, source_target_pairs={{32,0},{64,32},{96,64},{128,96},{160,128},{192,160},{224,192},{256... | collective-permute-start | bytes 24584 | tf_op jit(solution)/shard_map/ppermute | solution.py:15
  83.6 11.1 %collective-permute-start.11 = (f32[16,10,1]{2,1,0:T(8,128)S(1)}, f32[16,10,1]{2,1,0:T(8,128)S(1)}, u32[]{:S(2)}, u32[]{:S(2)}) collective-permute-start(f32[16,10,1]{2,1,0:T(8,128)S(1)} %get-tuple-element.32), channel_id=1, source_target_pairs={{1,0},{2,1},{3,2},{4,3},{5,4},{6,5},{7,6},{8,7},{9,8},{10,9},{11,1... | collective-permute-start | bytes 1928 | tf_op jit(solution)/shard_map/ppermute | solution.py:15
  85.5 12.3 %copy-start.1 = (f32[16,16,256]{2,1,0:T(8,128)S(1)}, f32[16,16,256]{2,1,0:T(8,128)}, u32[]{:S(2)}) copy-start(f32[16,16,256]{2,1,0:T(8,128)} %param.15) | copy-start | bytes 786436
  88.0 8.6 %collective-permute-start.10 = (f32[16,10,1]{2,1,0:T(8,128)S(1)}, f32[16,10,1]{2,1,0:T(8,128)S(1)}, u32[]{:S(2)}, u32[]{:S(2)}) collective-permute-start(f32[16,10,1]{2,1,0:T(8,128)S(1)} %get-tuple-element.33), channel_id=1, source_target_pairs={{0,1},{1,2},{2,3},{3,4},{4,5},{5,6},{6,7},{7,8},{8,9},{9,10},{10,1... | collective-permute-start | bytes 1928 | tf_op jit(solution)/shard_map/ppermute | solution.py:12
  98.8 12.2 %collective-permute-start.14 = (f32[16,20,2]{2,1,0:T(8,128)S(1)}, f32[16,20,2]{2,1,0:T(8,128)S(1)}, u32[]{:S(2)}, u32[]{:S(2)}) collective-permute-start(f32[16,20,2]{2,1,0:T(8,128)S(1)} %get-tuple-element.20), channel_id=1, source_target_pairs={{0,1},{1,2},{2,3},{3,4},{4,5},{5,6},{6,7},{7,8},{8,9},{9,10},{10,1... | collective-permute-start | bytes 7688 | tf_op jit(solution)/shard_map/ppermute | solution.py:12
  105.9 11.3 %collective-permute-start.15 = (f32[16,20,2]{2,1,0:T(8,128)S(1)}, f32[16,20,2]{2,1,0:T(8,128)}, u32[]{:S(2)}, u32[]{:S(2)}) collective-permute-start(f32[16,20,2]{2,1,0:T(8,128)S(1)} %get-tuple-element.21), channel_id=1, source_target_pairs={{1,0},{2,1},{3,2},{4,3},{5,4},{6,5},{7,6},{8,7},{9,8},{10,9},{11,1... | collective-permute-start | bytes 7688 | tf_op jit(solution)/shard_map/ppermute | solution.py:15
  111.0 0.7 copy-start.5
  123.0 4.8 %copy-start.13 = (f32[3,4,9]{2,1,0:T(4,128)S(1)}, f32[3,4,9]{2,1,0:T(4,128)}, u32[]{:S(2)}) copy-start(f32[3,4,9]{2,1,0:T(4,128)} %param.12) | copy-start | bytes 1300
  127.8 12.0 %copy-start.11 = (f32[3,4,4]{2,1,0:T(4,128)S(1)}, f32[3,4,4]{2,1,0:T(4,128)}, u32[]{:S(2)}) copy-start(f32[3,4,4]{2,1,0:T(4,128)} %param.13) | copy-start | bytes 580
  130.0 19.1 %copy-start.4 = (f32[16,16]{1,0:T(8,128)S(1)}, f32[16,16]{1,0:T(8,128)}, u32[]{:S(2)}) copy-start(f32[16,16]{1,0:T(8,128)} %param.14) | copy-start | bytes 3076
  131.1 9.4 %collective-permute-start.16 = (f32[16,2,128]{2,1,0:T(2,128)S(1)}, f32[16,2,128]{2,1,0:T(2,128)S(1)}, u32[]{:S(2)}, u32[]{:S(2)}) collective-permute-start(f32[16,2,128]{2,1,0:T(2,128)S(1)} %get-tuple-element.38), channel_id=1, source_target_pairs={{0,32},{32,64},{64,96},{96,128},{128,160},{160,192},{192,224},{224... | collective-permute-start | bytes 49160 | tf_op jit(solution)/shard_map/ppermute | solution.py:12
  137.4 6.3 %collective-permute-start.17 = (f32[16,2,128]{2,1,0:T(2,128)S(1)}, f32[16,2,128]{2,1,0:T(2,128)S(1)}, u32[]{:S(2)}, u32[]{:S(2)}) collective-permute-start(f32[16,2,128]{2,1,0:T(2,128)S(1)} %get-tuple-element.39), channel_id=1, source_target_pairs={{32,0},{64,32},{96,64},{128,96},{160,128},{192,160},{224,192},{256... | collective-permute-start | bytes 49160 | tf_op jit(solution)/shard_map/ppermute | solution.py:15
  143.8 6.5 %collective-permute-start.18 = (f32[16,12,2]{2,1,0:T(8,128)S(1)}, f32[16,12,2]{2,1,0:T(8,128)S(1)}, u32[]{:S(2)}, u32[]{:S(2)}) collective-permute-start(f32[16,12,2]{2,1,0:T(8,128)S(1)} %get-tuple-element.30), channel_id=1, source_target_pairs={{0,1},{1,2},{2,3},{3,4},{4,5},{5,6},{6,7},{7,8},{8,9},{9,10},{10,1... | collective-permute-start | bytes 4616 | tf_op jit(solution)/shard_map/ppermute | solution.py:12
  145.8 9.0 %collective-permute-start.19 = (f32[16,12,2]{2,1,0:T(8,128)S(1)}, f32[16,12,2]{2,1,0:T(8,128)S(1)}, u32[]{:S(2)}, u32[]{:S(2)}) collective-permute-start(f32[16,12,2]{2,1,0:T(8,128)S(1)} %get-tuple-element.31), channel_id=1, source_target_pairs={{1,0},{2,1},{3,2},{4,3},{5,4},{6,5},{7,6},{8,7},{9,8},{10,9},{11,1... | collective-permute-start | bytes 4616 | tf_op jit(solution)/shard_map/ppermute | solution.py:15
  157.8 5.7 %collective-permute-start.20 = (f32[16,2,64]{2,1,0:T(2,128)S(1)}, f32[16,2,64]{2,1,0:T(2,128)S(1)}, u32[]{:S(2)}, u32[]{:S(2)}) collective-permute-start(f32[16,2,64]{2,1,0:T(2,128)S(1)} %get-tuple-element.52), channel_id=1, source_target_pairs={{0,32},{32,64},{64,96},{96,128},{128,160},{160,192},{192,224},{224... | collective-permute-start | bytes 24584 | tf_op jit(solution)/shard_map/ppermute | solution.py:12
  161.0 6.3 %collective-permute-start.21 = (f32[16,2,64]{2,1,0:T(2,128)S(1)}, f32[16,2,64]{2,1,0:T(2,128)S(1)}, u32[]{:S(2)}, u32[]{:S(2)}) collective-permute-start(f32[16,2,64]{2,1,0:T(2,128)S(1)} %get-tuple-element.53), channel_id=1, source_target_pairs={{32,0},{64,32},{96,64},{128,96},{160,128},{192,160},{224,192},{256... | collective-permute-start | bytes 24584 | tf_op jit(solution)/shard_map/ppermute | solution.py:15
  167.4 6.4 %collective-permute-start.22 = (f32[16,8,2]{2,1,0:T(8,128)S(1)}, f32[16,8,2]{2,1,0:T(8,128)S(1)}, u32[]{:S(2)}, u32[]{:S(2)}) collective-permute-start(f32[16,8,2]{2,1,0:T(8,128)S(1)} %get-tuple-element.36), channel_id=1, source_target_pairs={{0,1},{1,2},{2,3},{3,4},{4,5},{5,6},{6,7},{7,8},{8,9},{9,10},{10,1... | collective-permute-start | bytes 3080 | tf_op jit(solution)/shard_map/ppermute | solution.py:12
  169.3 8.3 %collective-permute-start.23 = (f32[16,8,2]{2,1,0:T(8,128)S(1)}, f32[16,8,2]{2,1,0:T(8,128)S(1)}, u32[]{:S(2)}, u32[]{:S(2)}) collective-permute-start(f32[16,8,2]{2,1,0:T(8,128)S(1)} %get-tuple-element.37), channel_id=1, source_target_pairs={{1,0},{2,1},{3,2},{4,3},{5,4},{6,5},{7,6},{8,7},{9,8},{10,9},{11,1... | collective-permute-start | bytes 3080 | tf_op jit(solution)/shard_map/ppermute | solution.py:15
where the time goes:
time: 181 us; the launch traced here: 180 us
  starting transfers between devices  83.3 us (46%)
  waiting for transfers between devices  33.5 us (19%)
  local copies, waits for them, and re-layouts  32.9 us (18%)
  matrix products  21.4 us (12%)
  other arithmetic  7.32 us (4%)
    ppermute x12, starting transfers between devices, with_halo(): lax.ppermute(lax.slice_in_dim(block, block.shape[dim] - width, None, axis...  55.5 us
    ppermute x12, waiting for transfers between devices, with_halo(): lax.ppermute(lax.slice_in_dim(block, 0, width, axis=dim), axis, backward)  31.8 us
    ppermute x12, starting transfers between devices, with_halo(): lax.ppermute(lax.slice_in_dim(block, 0, width, axis=dim), axis, backward)  27.8 us
    unnamed x40, local copies, waits for them, and re-layouts  8.58 us
    transpose x9, local copies, waits for them, and re-layouts, to_blocks(): return field.reshape(chans, rows // 2, 2, cols // 2, 2).transpose(2, 4, 0...  8.16 us
    dot_general x4, matrix products, mix_channels(): jnp.einsum('cd,dij->cij', factor, field, precision=lax.Precision.HIGHEST)  5.72 us
    dot_general x4, matrix products, mix_transposed(): jnp.einsum('dc,dij->cij', factor, field, precision=lax.Precision.HIGHEST)  4.68 us
    concatenate x14, other arithmetic, with_halo(): block = jnp.concatenate([low, block, high], axis=dim)  4.3 us
  transfers between devices with their start and end apart: 24, of which 9 were waited for; matrix products, arithmetic and copies ran while one was open for 21% of the time, Pallas kernels for 0%

commit v1 on v0

v1 whole, which is shorter than its diff:
```python
import jax
import jax.numpy as jnp
from jax import lax
from jax.experimental import pallas as pl
from jax.experimental.pallas import tpu as pltpu
from jax.sharding import PartitionSpec as P

F32 = jnp.float32
CH = 16
COLS = (32, 64, 128, 256)
ROWS = (2, 4, 8, 16)
WIDE = (128, 128, 256, 256)
VMEM_LIMIT = 40 * 1024 * 1024


def iota(shape, dim):
    return lax.broadcasted_iota(jnp.int32, shape, dim)


def mul(left, right):
    return lax.dot_general(
        left, right, (((1,), (0,)), ((), ())),
        precision=lax.Precision.HIGHEST, preferred_element_type=F32,
    )


def mul_t(left, right):
    return lax.dot_general(
        left, right, (((1,), (1,)), ((), ())),
        precision=lax.Precision.HIGHEST, preferred_element_type=F32,
    )


def col_of(lane, cols, none):
    return jnp.where(
        lane < cols,
        lane,
        jnp.where(lane < cols + 2, lane - cols - 2, jnp.where(lane < cols + 4, lane - 2, none)),
    )


def refine_matrix(weights, level):
    fine, coarse = WIDE[level], WIDE[level - 1]
    fine_col = col_of(iota((fine // 8, 8, coarse), 0) * 8 + iota((fine // 8, 8, coarse), 1), COLS[level], -4096)
    coarse_col = col_of(iota((fine // 8, 8, coarse), 2), COLS[level - 1], 4096)
    step = coarse_col - (fine_col >> 1)
    odd = iota((1, 8, coarse), 1) & 1
    bands = []
    for a in (0, 1):
        parts = []
        for da in (0, 1, 2):
            block = jnp.zeros((fine // 8, 8, coarse), F32)
            for db in (0, 1, 2):
                n = 3 * da + db
                pair = jnp.where(odd == 0, weights[level - 1, 2 * a, n], weights[level - 1, 2 * a + 1, n])
                block = jnp.where(step == db - 1, pair, block)
            parts.append(block.reshape(fine, coarse))
        bands.append(jnp.concatenate(parts, axis=1))
    return jnp.concatenate(bands, axis=0)


def push(rows, matrix, level):
    blocks = len(rows) - 2
    left = jnp.concatenate(
        [jnp.concatenate(rows[da : da + blocks], axis=0) for da in (0, 1, 2)], axis=1
    )
    return mul_t(left, matrix)


def push_rows(rows, matrix, level):
    fine = WIDE[level]
    out = push(rows, matrix, level)
    result = []
    for i in range(len(rows) - 2):
        for a in (0, 1):
            result.append(out[CH * i : CH * (i + 1), fine * a : fine * (a + 1)])
    return result


def pull(left, matrix, level, blocks):
    coarse = WIDE[level - 1]
    out = mul(left, matrix)
    result = []
    for i in range(-1, blocks + 1):
        total = None
        for da in (0, 1, 2):
            block = i - (da - 1)
            if 0 <= block < blocks:
                term = out[CH * block : CH * (block + 1), coarse * da : coarse * (da + 1)]
                total = term if total is None else total + term
        result.append(total)
    return result


def pull_rows(rows, matrix, level):
    blocks = len(rows) // 2
    left = jnp.concatenate(
        [jnp.concatenate([rows[2 * i + a] for i in range(blocks)], axis=0) for a in (0, 1)], axis=1
    )
    return pull(left, matrix, level, blocks)


def swap_lanes(x):
    axis = x.ndim - 1
    lane = iota(x.shape, axis)
    return jnp.where((lane & 1) == 0, pltpu.roll(x, x.shape[axis] - 1, axis), pltpu.roll(x, 1, axis))


def factor_rows(rows, factor, level, transposed):
    odd = iota(rows[0].shape, 1) & 1
    swapped = [swap_lanes(r) for r in rows]

    def entry(a, b, a2, b2):
        if transposed:
            return factor[level - 1, 2 * a2 + b2, 2 * a + b]
        return factor[level - 1, 2 * a + b, 2 * a2 + b2]

    result = []
    for i in range(len(rows) // 2):
        for a in (0, 1):
            total = None
            for a2 in (0, 1):
                same = jnp.where(odd == 0, entry(a, 0, a2, 0), entry(a, 1, a2, 1))
                other = jnp.where(odd == 0, entry(a, 0, a2, 1), entry(a, 1, a2, 0))
                term = same * rows[2 * i + a2] + other * swapped[2 * i + a2]
                total = term if total is None else total + term
            result.append(total)
    return result


def factor_tile(x, factor, transposed):
    odd_row = iota((1, 8, 128), 1) & 1
    odd_col = iota((1, 8, 128), 2) & 1
    side = swap_lanes(x)

    def swap_rows(y):
        row = iota(y.shape, 1)
        return jnp.where((row & 1) == 0, pltpu.roll(y, 7, 1), pltpu.roll(y, 1, 1))

    def coefficient(flip_row, flip_col):
        values = []
        for a in (0, 1):
            for b in (0, 1):
                here, there = 2 * a + b, 2 * (a ^ flip_row) + (b ^ flip_col)
                values.append(factor[2, there, here] if transposed else factor[2, here, there])
        return jnp.where(
            odd_row == 0,
            jnp.where(odd_col == 0, values[0], values[1]),
            jnp.where(odd_col == 0, values[2], values[3]),
        )

    return (
        coefficient(0, 0) * x
        + coefficient(0, 1) * side
        + coefficient(1, 0) * swap_rows(x)
        + coefficient(1, 1) * swap_rows(side)
    )


def spread_factor(mixing):
    return mul(jnp.where(iota((256, CH), 0) // CH == iota((256, CH), 1), 1.0, 0.0), mixing)


def mix_sorted(mixing):
    spread = spread_factor(mixing)
    tiled = jnp.where((iota((256, CH), 0) & 15) == iota((256, CH), 1), 1.0, 0.0)
    full = mul_t(spread, tiled)
    row = iota((256, 256), 0) & 15
    col = iota((256, 256), 1)
    return jnp.where(row == 2 * ((col & 127) >> 4) + (col >> 7), full, 0.0)


def mix_sorted_t(mixing):
    spread = spread_factor(mixing)
    tiled = jnp.where((iota((256, CH), 0) & 15) == iota((256, CH), 1), 1.0, 0.0)
    full = mul_t(tiled, spread)
    col = iota((256, 256), 1) & 15
    row = iota((256, 256), 0)
    return jnp.where(col == 2 * ((row & 127) >> 4) + (row >> 7), full, 0.0)


def edge_mask(width, cols, at_left, at_right):
    lane = iota((1, width), 1)
    left = jnp.where((lane >= cols) & (lane < cols + 2), at_left, 0)
    right = jnp.where((lane >= cols + 2) & (lane < cols + 4), at_right, 0)
    return jnp.where(left + right > 0, 0.0, 1.0)


def clear_outside(rows, before, after, place, grid, level, width):
    ty, tx = place
    cols = edge_mask(
        width, COLS[level], (tx == 0).astype(jnp.int32), (tx == grid[1] - 1).astype(jnp.int32)
    )
    top = jnp.where(ty == 0, 0.0, 1.0)
    bottom = jnp.where(ty == grid[0] - 1, 0.0, 1.0)
    result = []
    for k, row in enumerate(rows):
        mask = cols
        if k < before:
            mask = cols * top
        elif k >= len(rows) - after:
            mask = cols * bottom
        result.append(row * mask)
    return result


def wide(x, width):
    if x.shape[1] == width:
        return x
    return jnp.concatenate([x, jnp.zeros((x.shape[0], width - x.shape[1]), F32)], axis=1)


def move(x, source, target, lane):
    shift = (target - source) % 128
    moved = pltpu.roll(x, shift, 1) if shift else x
    return jnp.where((lane >= target) & (lane < target + 2), moved, 0.0)


def gather_lanes(pieces, lane):
    total = jnp.zeros((CH, 128), F32)
    for k, (x, source) in enumerate(pieces):
        shift = (2 * k - source) % 128
        moved = pltpu.roll(x, shift, 1) if shift else x
        total = jnp.where((lane >= 2 * k) & (lane < 2 * k + 2), moved, total)
    return total


def halo_tile(x, level):
    return x[:, 128:] if level == 2 else x


def first_kernel(grid):
    def body(weights, factor, place_ref, mixing, cot, e0, e1, e2, send_a, send_b, g0, g1, g2, u0, u1, u2):
        place = (place_ref[0], place_ref[1])
        lane = iota((CH, 128), 1)
        pixels = mul(mix_sorted_t(mixing[...]), cot[...].reshape(256, 256))
        left = jnp.concatenate([pixels[:128], pixels[128:]], axis=1)
        ups = [None, None, None]
        ups[2] = pull(left, refine_matrix(weights, 3), 3, 8)
        ups[2] = clear_outside(ups[2], 1, 1, place, grid, 2, 256)
        none = jnp.zeros((CH, 256), F32)
        ups[1] = pull_rows([none] + ups[2] + [none], refine_matrix(weights, 2), 2)
        ups[1] = clear_outside(ups[1], 2, 2, place, grid, 1, 128)
        ups[0] = pull_rows(ups[1], refine_matrix(weights, 1), 1)
        gs = [[wide(e0[:, r, :], 128) for r in range(2)]]
        gs.append(factor_rows([wide(e1[:, r, :], 128) for r in range(4)], factor, 1, False))
        gs.append(factor_rows([e2[:, r, :] for r in range(8)], factor, 2, False))
        high, low = [], []
        for level in (0, 1, 2):
            for row in gs[level]:
                high.append((row, COLS[level] - 2))
                low.append((row, 0))
        for level in (0, 1, 2):
            base = COLS[level] % 128
            for row in ups[level]:
                high.append((halo_tile(row, level), base + 2))
                low.append((halo_tile(row, level), base))
        high, low = gather_lanes(high, lane), gather_lanes(low, lane)
        even = (place[1] & 1) == 0
        send_a[...] = jnp.where(even, high, low)
        send_b[...] = jnp.where(even, low, high)
        for ref, rows in ((g0, gs[0]), (g1, gs[1]), (g2, gs[2]), (u0, ups[0]), (u1, ups[1]), (u2, ups[2])):
            for k, row in enumerate(rows):
                ref[k] = row[:, :128]

    return body


def second_kernel(grid):
    def body(place_ref, got_a, got_b, g0, g1, g2, u0, u1, u2, send_a, send_b, x0, x1, x2, v0, v1, v2):
        ty, tx = place_ref[0], place_ref[1]
        lane = iota((CH, 128), 1)
        even = (tx & 1) == 0
        from_right = jnp.where(even, got_a[...], got_b[...])
        from_left = jnp.where(even, got_b[...], got_a[...])
        k = 0
        wides, ups = [], []
        for level, ref in ((0, g0), (1, g1), (2, g2)):
            rows = []
            for r in range(ROWS[level]):
                base = COLS[level] % 128
                halo = move(from_left, 2 * k, base, lane) + move(from_right, 2 * k, base + 2, lane)
                rows.append([ref[r], halo] if level == 2 else [ref[r] + halo])
                k += 1
            wides.append(rows)
        for level, ref in ((0, u0), (1, u1), (2, u2)):
            rows = []
            for r in range(ref.shape[0]):
                rows.append(
                    ref[r] + move(from_left, 2 * k, 0, lane) + move(from_right, 2 * k, COLS[level] - 2, lane)
                )
                k += 1
            ups.append(rows)
        low = [t for level in (0, 1, 2) for row in wides[level][:2] for t in row]
        high = [t for level in (0, 1, 2) for row in wides[level][-2:] for t in row]
        low += ups[0][:2] + ups[1][:2] + ups[2][:1]
        high += ups[0][-2:] + ups[1][-2:] + ups[2][-1:]
        even = (ty & 1) == 0
        for j in range(len(low)):
            send_a[j] = jnp.where(even, high[j], low[j])
            send_b[j] = jnp.where(even, low[j], high[j])
        for ref, rows in ((x0, wides[0]), (x1, wides[1]), (x2, wides[2])):
            for j, row in enumerate(rows):
                ref[j] = row[0] if len(row) == 1 else jnp.concatenate(row, axis=1)
        for ref, rows, trim in ((v0, ups[0], 2), (v1, ups[1], 2), (v2, ups[2], 1)):
            for j in range(ref.shape[0]):
                ref[j] = rows[j + trim]

    return body


def third_kernel(grid):
    def body(weights, factor, place_ref, mixing, got_a, got_b, x0, x1, x2, v0, v1, v2, local, sky, d0, d1, d2):
        place = (place_ref[0], place_ref[1])
        even = (place[0] & 1) == 0

        def pick(j):
            first, second = got_a[j], got_b[j]
            return jnp.where(even, second, first), jnp.where(even, first, second)

        tiles = [pick(j) for j in range(13)]
        above, below = [t[0] for t in tiles], [t[1] for t in tiles]

        def join(parts):
            return [jnp.concatenate(parts[0:2], axis=1), jnp.concatenate(parts[2:4], axis=1)]

        field = above[0:2] + [x0[r] for r in range(2)] + below[0:2]
        mixed = above[2:4] + [x1[r] for r in range(4)] + below[2:4]
        field = push_rows(field, refine_matrix(weights, 1), 1)
        field = [f + m for f, m in zip(field, mixed)]
        field = clear_outside(field, 2, 2, place, grid, 1, 128)
        mixed = join(above[4:8]) + [x2[r] for r in range(8)] + join(below[4:8])
        field = push_rows(field, refine_matrix(weights, 2), 2)
        field = [f + m for f, m in zip(field, mixed)]
        field = clear_outside(field, 2, 2, place, grid, 2, 256)
        fine = push(field[1:11], refine_matrix(weights, 3), 3)
        fine = jnp.concatenate([fine[:, :256], fine[:, 256:]], axis=0)
        sky[...] = (mul(mix_sorted(mixing[...]), fine) + local[...]).reshape(CH, 16, 256)
        up0 = [v0[r] + above[8 + r] + below[8 + r] for r in range(2)]
        up1 = [v1[r] for r in range(4)]
        up1 = [up1[0] + above[10], up1[1] + above[11], up1[2] + below[10], up1[3] + below[11]]
        up2 = [v2[r] for r in range(8)]
        up2[0] = up2[0] + above[12]
        up2[7] = up2[7] + below[12]
        up1 = factor_rows(up1, factor, 1, True)
        up2 = factor_rows(up2, factor, 2, True)
        for ref, rows, cols in ((d0, up0, 32), (d1, up1, 64), (d2, up2, 128)):
            for r, row in enumerate(rows):
                ref[:, r, :] = row[:, :cols]

    return body


def local_body(factor, mixing, cot, e3, local, grad):
    spread = spread_factor(mixing[...])
    column = jnp.where(iota((256, CH), 0) // CH == iota((256, CH), 1), 1.0, 0.0)
    same = (iota((256, 256), 0) & 15) == (iota((256, 256), 1) & 15)

    def factored(ref, transposed):
        halves = [
            factor_tile(ref[:, :, 128 * h : 128 * (h + 1)].reshape(32, 8, 128), factor, transposed).reshape(256, 128)
            for h in (0, 1)
        ]
        return jnp.concatenate(halves, axis=1)

    grad[...] = mul(jnp.where(same, mul_t(column, spread), 0.0), factored(cot, True)).reshape(CH, 16, 256)
    local[...] = mul(jnp.where(same, mul_t(spread, column), 0.0), factored(e3, False))


def swaps(count, first):
    pairs = []
    for i in range(first, count - 1, 2):
        pairs += [(i, i + 1), (i + 1, i)]
    return pairs


def shaped(*shape):
    return jax.ShapeDtypeStruct(shape, F32)


SMEM = pl.BlockSpec(memory_space=pltpu.SMEM)
VMEM = pl.BlockSpec(memory_space=pltpu.VMEM)


def call(body, specs, outs, args):
    return pl.pallas_call(
        body,
        out_shape=outs,
        in_specs=specs,
        out_specs=[VMEM] * len(outs),
        compiler_params=pltpu.CompilerParams(vmem_limit_bytes=VMEM_LIMIT),
    )(*args)


def device_body(grid):
    def on_device(e0, e1, e2, e3, weights, factor, mixing, cot):
        place = jnp.stack([lax.axis_index("ty"), lax.axis_index("tx")]).astype(jnp.int32)
        rows = [shaped(2, CH, 128), shaped(4, CH, 128), shaped(8, CH, 128)]
        ups = [shaped(6, CH, 128), shaped(8, CH, 128), shaped(10, CH, 128)]
        first = call(
            first_kernel(grid),
            [SMEM] * 3 + [VMEM] * 5,
            [shaped(CH, 128)] * 2 + rows + ups,
            (weights, factor, place, mixing, cot, e0, e1, e2),
        )
        got_a = lax.ppermute(first[0], "tx", swaps(grid[1], 0))
        got_b = lax.ppermute(first[1], "tx", swaps(grid[1], 1))
        second = call(
            second_kernel(grid),
            [SMEM] + [VMEM] * 8,
            [shaped(13, CH, 128)] * 2 + [shaped(2, CH, 128), shaped(4, CH, 128), shaped(8, CH, 256)] + rows,
            (place, got_a, got_b, *first[2:]),
        )
        local, grad3 = call(
            local_body,
            [SMEM] + [VMEM] * 3,
            [shaped(256, 256), shaped(CH, 16, 256)],
            (factor, mixing, cot, e3),
        )
        got_a = lax.ppermute(second[0], "ty", swaps(grid[0], 0))
        got_b = lax.ppermute(second[1], "ty", swaps(grid[0], 1))
        sky, grad0, grad1, grad2 = call(
            third_kernel(grid),
            [SMEM] * 3 + [VMEM] * 10,
            [shaped(CH, 16, 256), shaped(CH, 2, 32), shaped(CH, 4, 64), shaped(CH, 8, 128)],
            (weights, factor, place, mixing, got_a, got_b, *second[2:], local),
        )
        return (sky, grad0, grad1, grad2, grad3)

    return on_device


def solution(mesh):
    tiles = P(None, "ty", "tx")
    return jax.shard_map(
        device_body((mesh.shape["ty"], mesh.shape["tx"])),
        mesh=mesh,
        in_specs=(tiles, tiles, tiles, tiles, P(), P(), P(), tiles),
        out_specs=(tiles,) * 5,
        check_vma=False,
    )
```

time: 181 us -> 39.6 us (0.22)
  the two profiles are of different devices: /device:TPU:223 before, /device:TPU:225 now
where the time goes in v1:
time: 39.6 us; the launch traced here: 39.1 us
  starting transfers between devices  16 us (40%)
  Pallas kernels  13.7 us (35%)
  local copies, waits for them, and re-layouts  4.58 us (12%)
  waiting for transfers between devices  4.09 us (10%)
  between operations  0.74 us (2%)
    pallas_call x4, Pallas kernels, call(): pl.pallas_call(body, out_shape=outs, in_specs=specs, out_specs=[VMEM] * l...  13.7 us
    ppermute x1, starting transfers between devices, on_device(): got_b = lax.ppermute(second[1], 'ty', swaps(grid[0], 1))  5.11 us
    unnamed x18, local copies, waits for them, and re-layouts  4.58 us
    ppermute x1, waiting for transfers between devices, on_device(): got_b = lax.ppermute(first[1], 'tx', swaps(grid[1], 1))  4.09 us
    ppermute x1, starting transfers between devices, on_device(): got_a = lax.ppermute(second[0], 'ty', swaps(grid[0], 0))  4.01 us
    ppermute x1, starting transfers between devices, on_device(): got_b = lax.ppermute(first[1], 'tx', swaps(grid[1], 1))  3.61 us
    ppermute x1, starting transfers between devices, on_device(): got_a = lax.ppermute(first[0], 'tx', swaps(grid[1], 0))  3.25 us
  transfers between devices with their start and end apart: 4, of which 1 were waited for; matrix products, arithmetic and copies ran while one was open for 0% of the time, Pallas kernels for 7%

profile of v1, /device:TPU:225, one launch (start us, length us, event | category | flops | bytes accessed | tf_op | source)
XLA Modules:
  0.0 39.1 jit_solution(7476225930243089447)
XLA Ops:
  0.6 0.0 copy-start.3
  0.6 0.0 copy-start.5
  0.7 0.1 pad_add_fusion.place_ref
  0.7 0.6 %copy-done.3 = f32[16,16]{1,0:T(8,128)S(1)} copy-done((f32[16,16]{1,0:T(8,128)S(1)}, f32[16,16]{1,0:T(8,128)}, u32[]{:S(2)}) %copy-start.3) | copy-done | bytes 1048
  1.3 0.0 copy-done.5
  1.3 0.0 copy-start
  1.3 0.9 %copy-done = f32[16,16,256]{2,1,0:T(8,128)S(1)} copy-done((f32[16,16,256]{2,1,0:T(8,128)S(1)}, f32[16,16,256]{2,1,0:T(8,128)}, u32[]{:S(2)}) %copy-start) | copy-done | bytes 262168
  2.3 0.0 copy-start.4
  2.3 0.8 %copy-done.4 = f32[16,8,128]{2,1,0:T(8,128)S(1)} copy-done((f32[16,8,128]{2,1,0:T(8,128)S(1)}, f32[16,8,128]{2,1,0:T(8,128)}, u32[]{:S(2)}) %copy-start.4) | copy-done | bytes 65560
  3.1 0.0 copy-start.6
  3.1 0.8 %copy-done.6 = f32[16,4,64]{2,1,0:T(4,128)S(1)} copy-done((f32[16,4,64]{2,1,0:T(4,128)S(1)}, f32[16,4,64]{2,1,0:T(4,128)}, u32[]{:S(2)}) %copy-start.6) | copy-done | bytes 16408
  3.9 0.0 copy-start.7
  3.9 0.7 %copy-done.7 = f32[3,4,9]{2,1,0:T(4,128)S(1)} copy-done((f32[3,4,9]{2,1,0:T(4,128)S(1)}, f32[3,4,9]{2,1,0:T(4,128)}, u32[]{:S(2)}) %copy-start.7) | copy-done | bytes 456
  4.6 0.0 copy-start.8
  4.6 0.7 %copy-done.8 = f32[16,2,32]{2,1,0:T(2,128)S(1)} copy-done((f32[16,2,32]{2,1,0:T(2,128)S(1)}, f32[16,2,32]{2,1,0:T(2,128)}, u32[]{:S(2)}) %copy-start.8) | copy-done | bytes 4120
  5.3 0.0 copy-start.2
  5.3 4.7 %shard_map.119 = (f32[16,128]{1,0:T(8,128)S(1)}, f32[16,128]{1,0:T(8,128)S(1)}, f32[2,16,128]{2,1,0:T(8,128)S(1)}, f32[4,16,128]{2,1,0:T(8,128)S(1)}, f32[8,16,1...) custom-call(f32[3,4,9]{2,1,0:T(4,128)S(1)} %copy-done.7, ...), custom_call_target="tpu_custom_call" | custom-call | tf_op jit(solution)/shard_map/pallas_call | solution.py:386
  10.0 0.0 copy-start.1
  10.0 3.3 %collective-permute-start = (f32[16,128]{1,0:T(8,128)S(1)}, f32[16,128]{1,0:T(8,128)S(1)}, u32[]{:S(2)}, u32[]{:S(2)}) collective-permute-start(f32[16,128]{1,0:T(8,128)S(1)} %get-tuple-element.27), channel_id=1, source_target_pairs={{0,1},{1,0},{2,3},{3,2},{4,5},{5,4},{6,7},{7,6},{8,9},{9,8},{10,11... | collective-permute-start | bytes 24584 | tf_op jit(solution)/shard_map/ppermute | solution.py:406
  13.2 3.6 %collective-permute-start.1 = (f32[16,128]{1,0:T(8,128)S(1)}, f32[16,128]{1,0:T(8,128)S(1)}, u32[]{:S(2)}, u32[]{:S(2)}) collective-permute-start(f32[16,128]{1,0:T(8,128)S(1)} %get-tuple-element.28), channel_id=1, source_target_pairs={{1,2},{2,1},{3,4},{4,3},{5,6},{6,5},{7,8},{8,7},{9,10},{10,9},{11,... | collective-permute-start | bytes 24584 | tf_op jit(solution)/shard_map/ppermute | solution.py:407
  16.9 0.0 collective-permute-done.got_a
  16.9 4.1 %collective-permute-done.1.got_b = f32[16,128]{1,0:T(8,128)S(1)} collective-permute-done((f32[16,128]{1,0:T(8,128)S(1)}, f32[16,128]{1,0:T(8,128)S(1)}, u32[]{:S(2)}, u32[]{:S(2)}) %collective-permute-start.1) | collective-permute-done | bytes 8224 | tf_op jit(solution)/shard_map/ppermute | solution.py:407
  21.0 0.8 %shard_map.120 = (f32[13,16,128]{2,1,0:T(8,128)S(1)}, f32[13,16,128]{2,1,0:T(8,128)S(1)}, f32[2,16,128]{2,1,0:T(8,128)S(1)}, f32[4,16,128]{2,1,0:T(8,128)S(1)}, ...) custom-call(s32[2]{0:T(128)S(1)} %pad_add_fusion.place_ref, ...), custom_call_target="tpu_custom_call" | custom-call | tf_op jit(solution)/shard_map/pallas_call | solution.py:386
  21.7 4.0 %collective-permute-start.2 = (f32[13,16,128]{2,1,0:T(8,128)S(1)}, f32[13,16,128]{2,1,0:T(8,128)S(1)}, u32[]{:S(2)}, u32[]{:S(2)}) collective-permute-start(f32[13,16,128]{2,1,0:T(8,128)S(1)} %get-tuple-element.35), channel_id=1, source_target_pairs={{0,32},{32,0},{64,96},{96,64},{128,160},{160,128},{192,224},{224,1... | collective-permute-start | bytes 319496 | tf_op jit(solution)/shard_map/ppermute | solution.py:420
  25.7 5.1 %collective-permute-start.3 = (f32[13,16,128]{2,1,0:T(8,128)S(1)}, f32[13,16,128]{2,1,0:T(8,128)S(1)}, u32[]{:S(2)}, u32[]{:S(2)}) collective-permute-start(f32[13,16,128]{2,1,0:T(8,128)S(1)} %get-tuple-element.36), channel_id=1, source_target_pairs={{32,64},{64,32},{96,128},{128,96},{160,192},{192,160},{224,256},{2... | collective-permute-start | bytes 319496 | tf_op jit(solution)/shard_map/ppermute | solution.py:421
  30.8 0.0 copy-done.2
  30.9 0.0 copy-done.1
  30.9 2.6 %shard_map.121 = (f32[256,256]{1,0:T(8,128)S(1)}, f32[16,16,256]{2,1,0:T(8,128)}) custom-call(f32[3,4,4]{2,1,0:T(4,128)S(1)} %copy-done.5, f32[16,16]{1,0:T(8,128)S(1)} %copy-done.3, f32[16,16,256]{2,1,0:T(8,128)S(1)} %copy-done.1, f32[16,16,256]{2,1,0:T(8,128)S(1)} %copy-done.2), custom_call_target="tpu_custom_call" | custom-call | tf_op jit(solution)/shard_map/pallas_call | solution.py:386
  33.5 0.0 collective-permute-done.2.got_a
  33.5 0.0 collective-permute-done.3.got_b
  33.5 5.6 %shard_map.122 = (f32[16,16,256]{2,1,0:T(8,128)}, f32[16,2,32]{2,1,0:T(2,128)}, f32[16,4,64]{2,1,0:T(4,128)}, f32[16,8,128]{2,1,0:T(8,128)}) custom-call(f32[3,4,9]{2,1,0:T(4,128)S(1)} %copy-done.7, f32[3,4,4]{2,1,0:T(4,128)S(1)} %copy-done.5, s32[2]{0:T(128)S(1)} %pad_add_fusion.place_ref, f32[16,16]{1,0:T(8,128)S(1)} %copy-done.3, ...), custom_call_target="tpu_custom_call" | custom-call | tf_op jit(solution)/shard_map/pallas_call | solution.py:386
Async XLA Ops:
  0.6 0.7 %copy-start.3 = (f32[16,16]{1,0:T(8,128)S(1)}, f32[16,16]{1,0:T(8,128)}, u32[]{:S(2)}) copy-start(f32[16,16]{1,0:T(8,128)} %mixing.5) | copy-start | bytes 3076
  0.6 0.7 %copy-start.5 = (f32[3,4,4]{2,1,0:T(4,128)S(1)}, f32[3,4,4]{2,1,0:T(4,128)}, u32[]{:S(2)}) copy-start(f32[3,4,4]{2,1,0:T(4,128)} %factor.5) | copy-start | bytes 580
  1.3 0.9 %copy-start = (f32[16,16,256]{2,1,0:T(8,128)S(1)}, f32[16,16,256]{2,1,0:T(8,128)}, u32[]{:S(2)}) copy-start(f32[16,16,256]{2,1,0:T(8,128)} %cot.3) | copy-start | bytes 786436
  2.3 0.8 %copy-start.4 = (f32[16,8,128]{2,1,0:T(8,128)S(1)}, f32[16,8,128]{2,1,0:T(8,128)}, u32[]{:S(2)}) copy-start(f32[16,8,128]{2,1,0:T(8,128)} %e2.1) | copy-start | bytes 196612
  3.1 0.8 %copy-start.6 = (f32[16,4,64]{2,1,0:T(4,128)S(1)}, f32[16,4,64]{2,1,0:T(4,128)}, u32[]{:S(2)}) copy-start(f32[16,4,64]{2,1,0:T(4,128)} %e1.1) | copy-start | bytes 49156
  3.9 0.7 %copy-start.7 = (f32[3,4,9]{2,1,0:T(4,128)S(1)}, f32[3,4,9]{2,1,0:T(4,128)}, u32[]{:S(2)}) copy-start(f32[3,4,9]{2,1,0:T(4,128)} %weights.3) | copy-start | bytes 1300
  4.6 0.7 %copy-start.8 = (f32[16,2,32]{2,1,0:T(2,128)S(1)}, f32[16,2,32]{2,1,0:T(2,128)}, u32[]{:S(2)}) copy-start(f32[16,2,32]{2,1,0:T(2,128)} %e0.1) | copy-start | bytes 12292
  5.3 25.6 %copy-start.2 = (f32[16,16,256]{2,1,0:T(8,128)S(1)}, f32[16,16,256]{2,1,0:T(8,128)}, u32[]{:S(2)}) copy-start(f32[16,16,256]{2,1,0:T(8,128)} %e3.1) | copy-start | bytes 786436
  10.0 20.9 %copy-start.1 = (f32[16,16,256]{2,1,0:T(8,128)S(1)}, f32[16,16,256]{2,1,0:T(8,128)}, u32[]{:S(2)}) copy-start(f32[16,16,256]{2,1,0:T(8,128)} %cot.3) | copy-start | bytes 786436
  10.0 6.9 %collective-permute-start = (f32[16,128]{1,0:T(8,128)S(1)}, f32[16,128]{1,0:T(8,128)S(1)}, u32[]{:S(2)}, u32[]{:S(2)}) collective-permute-start(f32[16,128]{1,0:T(8,128)S(1)} %get-tuple-element.27), channel_id=1, source_target_pairs={{0,1},{1,0},{2,3},{3,2},{4,5},{5,4},{6,7},{7,6},{8,9},{9,8},{10,11... | collective-permute-start | bytes 24584 | tf_op jit(solution)/shard_map/ppermute | solution.py:406
  13.2 7.7 %collective-permute-start.1 = (f32[16,128]{1,0:T(8,128)S(1)}, f32[16,128]{1,0:T(8,128)S(1)}, u32[]{:S(2)}, u32[]{:S(2)}) collective-permute-start(f32[16,128]{1,0:T(8,128)S(1)} %get-tuple-element.28), channel_id=1, source_target_pairs={{1,2},{2,1},{3,4},{4,3},{5,6},{6,5},{7,8},{8,7},{9,10},{10,9},{11,... | collective-permute-start | bytes 24584 | tf_op jit(solution)/shard_map/ppermute | solution.py:407
  21.7 11.8 %collective-permute-start.2 = (f32[13,16,128]{2,1,0:T(8,128)S(1)}, f32[13,16,128]{2,1,0:T(8,128)S(1)}, u32[]{:S(2)}, u32[]{:S(2)}) collective-permute-start(f32[13,16,128]{2,1,0:T(8,128)S(1)} %get-tuple-element.35), channel_id=1, source_target_pairs={{0,32},{32,0},{64,96},{96,64},{128,160},{160,128},{192,224},{224,1... | collective-permute-start | bytes 319496 | tf_op jit(solution)/shard_map/ppermute | solution.py:420
  25.7 7.8 %collective-permute-start.3 = (f32[13,16,128]{2,1,0:T(8,128)S(1)}, f32[13,16,128]{2,1,0:T(8,128)S(1)}, u32[]{:S(2)}, u32[]{:S(2)}) collective-permute-start(f32[13,16,128]{2,1,0:T(8,128)S(1)} %get-tuple-element.36), channel_id=1, source_target_pairs={{32,64},{64,32},{96,128},{128,96},{160,192},{192,160},{224,256},{2... | collective-permute-start | bytes 319496 | tf_op jit(solution)/shard_map/ppermute | solution.py:421

commit v2 on v1

v2 whole, which is shorter than its diff:
```python
import jax
import jax.numpy as jnp
from jax import lax
from jax.experimental import pallas as pl
from jax.experimental.pallas import tpu as pltpu
from jax.sharding import PartitionSpec as P

F32 = jnp.float32
BF16 = jnp.bfloat16
CH = 16
COLS = (32, 64, 128, 256)
ROWS = (2, 4, 8, 16)
BASE = (64, 0, 0, 0)
HALO = (96, 100, 104)
VMEM_LIMIT = 40 * 1024 * 1024


def iota(shape, dim):
    return lax.broadcasted_iota(jnp.int32, shape, dim)


def dot(left, right, dims, precision=None):
    return lax.dot_general(
        left, right, (dims, ((), ())), precision=precision, preferred_element_type=F32
    )


NN = ((1,), (0,))
NT = ((1,), (1,))


def mul(left, right):
    return dot(left, right, NN, lax.Precision.HIGHEST)


def mul_t(left, right):
    return dot(left, right, NT, lax.Precision.HIGHEST)


def split(x):
    high = x.astype(BF16)
    return high, (x - high.astype(F32)).astype(BF16)


def mul3(left, right, dims):
    return (
        dot(left[0], right[0], dims) + (dot(left[1], right[0], dims) + dot(left[0], right[1], dims))
    )


def roll(x, shift):
    shift %= 128
    return pltpu.roll(x, shift, 1) if shift else x


def places():
    return lax.axis_index("ty"), lax.axis_index("tx")


def refine_weight(weights, level, fine_col, coarse_col, a, da):
    step = coarse_col - (fine_col >> 1)
    odd = iota((1, 8, coarse_col.shape[2]), 1) & 1
    block = jnp.zeros(step.shape, F32)
    for db in (0, 1, 2):
        n = 3 * da + db
        pair = jnp.where(odd == 0, weights[level - 1, 2 * a, n], weights[level - 1, 2 * a + 1, n])
        block = jnp.where(step == db - 1, pair, block)
    return block.reshape(step.shape[0] * 8, step.shape[2])


def fine_index(count):
    shape = (count // 8, 8, 128)
    return iota(shape, 0) * 8 + iota(shape, 1)


def lane_index(count):
    return iota((count // 8, 8, 128), 2)


def interior_col(lane, level, none):
    cols, base = COLS[level], BASE[level]
    return jnp.where((lane >= base) & (lane < base + cols), lane - base, none)


def halo_col(lane, level, place, none):
    step = lane - place
    return jnp.where(
        (step >= 0) & (step < 4), jnp.where(step < 2, step - 2, step - 2 + COLS[level]), none
    )


def both_col(lane, level, none):
    return interior_col(lane, level, halo_col(lane, level, HALO[level], none))


FAR, NEAR = -4096, 4096


def matrix_1(weights):
    fine, coarse = fine_index(128), lane_index(128)
    fine, coarse = both_col(fine, 1, FAR), both_col(coarse, 0, NEAR)
    return [[refine_weight(weights, 1, fine, coarse, a, da) for da in (0, 1, 2)] for a in (0, 1)]


def matrix_2(weights):
    index, coarse = fine_index(128), both_col(lane_index(128), 1, NEAR)
    inner = interior_col(index, 2, FAR)
    rows = [[refine_weight(weights, 2, inner, coarse, a, da) for da in (0, 1, 2)] for a in (0, 1)]
    halos = [halo_col(index, 2, HALO[2] + 4 * a, FAR) for a in (0, 1)]
    rows.append(
        [sum(refine_weight(weights, 2, halos[a], coarse, a, da) for a in (0, 1)) for da in (0, 1, 2)]
    )
    return rows


def matrix_3(weights):
    index, lane = fine_index(256), lane_index(256)
    inner = interior_col(lane, 2, NEAR)
    halos = [halo_col(lane, 2, HALO[2] + 4 * da, NEAR) for da in (0, 1, 2)]
    rows = []
    for a in (0, 1):
        row = [refine_weight(weights, 3, index, inner, a, da) for da in (0, 1, 2)]
        row.append(sum(refine_weight(weights, 3, index, halos[da], a, da) for da in (0, 1, 2)))
        rows.append(row)
    return rows


def store_matrix(blocks, high_ref, low_ref):
    down = 0
    for row in blocks:
        for j, block in enumerate(row):
            high, low = split(block)
            high_ref[down : down + block.shape[0], 128 * j : 128 * (j + 1)] = high
            low_ref[down : down + block.shape[0], 128 * j : 128 * (j + 1)] = low
        down += row[0].shape[0]


def stack(rows):
    return jnp.concatenate(rows, axis=0)


def beside(parts):
    return jnp.concatenate(parts, axis=1)


def block_sum(out, blocks, part):
    result = []
    for i in range(-1, blocks + 1):
        total = None
        for da in (0, 1, 2):
            block = i - (da - 1)
            if 0 <= block < blocks:
                term = part(out[CH * block : CH * (block + 1)], da)
                total = term if total is None else total + term
        result.append(total)
    return result


def tile(x, j):
    return x[:, 128 * j : 128 * (j + 1)]


def swap_lanes(x):
    axis = x.ndim - 1
    lane = iota(x.shape, axis)
    return jnp.where((lane & 1) == 0, pltpu.roll(x, x.shape[axis] - 1, axis), pltpu.roll(x, 1, axis))


def factor_rows(rows, factor, level, transposed):
    odd = iota(rows[0].shape, 1) & 1
    swapped = [swap_lanes(r) for r in rows]

    def entry(a, b, a2, b2):
        if transposed:
            return factor[level - 1, 2 * a2 + b2, 2 * a + b]
        return factor[level - 1, 2 * a + b, 2 * a2 + b2]

    pairs = {}
    for a in (0, 1):
        for a2 in (0, 1):
            pairs[a, a2] = (
                jnp.where(odd == 0, entry(a, 0, a2, 0), entry(a, 1, a2, 1)),
                jnp.where(odd == 0, entry(a, 0, a2, 1), entry(a, 1, a2, 0)),
            )
    result = []
    for i in range(len(rows) // 2):
        for a in (0, 1):
            total = None
            for a2 in (0, 1):
                same, other = pairs[a, a2]
                term = same * rows[2 * i + a2] + other * swapped[2 * i + a2]
                total = term if total is None else total + term
            result.append(total)
    return result


def factor_tile(x, factor, transposed):
    odd_row = iota((1, 8, 128), 1) & 1
    odd_col = iota((1, 8, 128), 2) & 1
    side = swap_lanes(x)

    def swap_rows(y):
        row = iota(y.shape, 1)
        return jnp.where((row & 1) == 0, pltpu.roll(y, 7, 1), pltpu.roll(y, 1, 1))

    def coefficient(flip_row, flip_col):
        values = []
        for a in (0, 1):
            for b in (0, 1):
                here, there = 2 * a + b, 2 * (a ^ flip_row) + (b ^ flip_col)
                values.append(factor[2, there, here] if transposed else factor[2, here, there])
        return jnp.where(
            odd_row == 0,
            jnp.where(odd_col == 0, values[0], values[1]),
            jnp.where(odd_col == 0, values[2], values[3]),
        )

    return (
        coefficient(0, 0) * x
        + coefficient(0, 1) * side
        + coefficient(1, 0) * swap_rows(x)
        + coefficient(1, 1) * swap_rows(side)
    )


def inside_mask(place, tx, last, keep_rest):
    lane = iota((1, 128), 1) - place
    left = jnp.where(tx == 0, 0.0, 1.0)
    right = jnp.where(tx == last, 0.0, 1.0)
    rest = jnp.full((1, 128), 1.0 if keep_rest else 0.0, F32)
    return jnp.where((lane >= 0) & (lane < 2), left, jnp.where((lane >= 2) & (lane < 4), right, rest))


def clear_outside(rows, around, mask, ty, last):
    top = jnp.where(ty == 0, 0.0, 1.0)
    bottom = jnp.where(ty == last, 0.0, 1.0)
    result = []
    for k, row in enumerate(rows):
        if k < around:
            row = row * (mask * top)
        elif k >= len(rows) - around:
            row = row * (mask * bottom)
        else:
            row = row * mask
        result.append(row)
    return result


def edge_col(lane, level, none):
    inside = (0, 2, 6, 16)[level]
    cols = COLS[level]
    if level == 3:
        return jnp.where(lane < 16, lane, jnp.where(lane < 32, cols + lane - 32, none))
    col = jnp.where(lane < 2, lane - 2, jnp.where(lane < 4, cols + lane - 2, none))
    col = jnp.where((lane >= 4) & (lane < 4 + inside), lane - 4, col)
    return jnp.where(
        (lane >= 4 + inside) & (lane < 4 + 2 * inside), cols - inside + lane - 4 - inside, col
    )


def edge_pull(rows, weights, level, width):
    blocks = len(rows) // 2
    fine = edge_col(fine_index(width), level, FAR)
    coarse = edge_col(lane_index(width), level - 1, NEAR)
    parts = []
    for da in (0, 1, 2):
        total = None
        for a in (0, 1):
            left = stack([rows[2 * i + a] for i in range(blocks)])[:, :width]
            term = mul(left, refine_weight(weights, level, fine, coarse, a, da))
            total = term if total is None else total + term
        parts.append(total)
    return block_sum(beside(parts), blocks, tile)


def widen(x):
    if x.shape[1] == 128:
        return x
    return beside([x, jnp.zeros((x.shape[0], 128 - x.shape[1]), F32)])


def first_kernel(grid):
    def body(weights_in, factor_in, cot_in, e0_in, e1_in, e2_in, send, weights, factor, cot, e0, e1, e2, edge, sems):
        copies = [
            pltpu.make_async_copy(source, target, sems.at[k])
            for k, (source, target) in enumerate(
                ((cot_in, cot), (weights_in, weights), (factor_in, factor), (e0_in, e0), (e1_in, e1), (e2_in, e2))
            )
        ]
        for copy in copies:
            copy.start()
        ty, tx = places()
        lane = iota((CH, 128), 1)
        for copy in copies[2:]:
            copy.wait()

        def edges(row, level):
            return jnp.where(lane < 2, row, roll(row, 4 - COLS[level]))

        pieces = [edges(widen(e0[:, r, :]), 0) for r in range(2)]
        pieces += factor_rows([edges(widen(e1[:, r, :]), 1) for r in range(4)], factor, 1, False)
        pieces += factor_rows([edges(e2[:, r, :], 2) for r in range(8)], factor, 2, False)
        for copy in copies[:2]:
            copy.wait()
        low = cot[:, :, :128].reshape(256, 128)
        high = cot[:, :, 128:].reshape(256, 128)
        edge[...] = jnp.where(iota((256, 128), 1) < 16, low, roll(high, 32))
        rows = [edge[pl.ds(r, CH, stride=16), :] for r in range(16)]
        mask = inside_mask(0, tx, grid[1] - 1, True)
        up2 = clear_outside(edge_pull(rows, weights, 3, 32), 1, mask, ty, grid[0] - 1)
        none = jnp.zeros((CH, 128), F32)
        up1 = edge_pull([none] + up2 + [none], weights, 2, 16)
        up1 = clear_outside(up1, 2, mask, ty, grid[0] - 1)
        up0 = edge_pull(up1, weights, 1, 8)
        pieces += up0 + up1 + up2
        totals = [none, none]
        for k, piece in enumerate(pieces):
            at = 4 * (k % 32)
            totals[k // 32] = jnp.where((lane >= at) & (lane < at + 4), roll(piece, at), totals[k // 32])
        send[0] = totals[0]
        send[1] = totals[1]

    return body


def inner_kernel(grid):
    def body(weights, factor, cot, e0, e1, e2, g0, g1, g2, u0, u1, u2, h1, l1, h2, l2, h3, l3, halves):
        ty, tx = places()
        store_matrix(matrix_3(weights), h3, l3)
        store_matrix(matrix_2(weights), h2, l2)
        store_matrix(matrix_1(weights), h1, l1)
        for r in range(2):
            g0[r] = roll(widen(e0[:, r, :]), BASE[0])
        for r, row in enumerate(factor_rows([widen(e1[:, r, :]) for r in range(4)], factor, 1, False)):
            g1[r] = row
        for r, row in enumerate(factor_rows([e2[:, r, :] for r in range(8)], factor, 2, False)):
            g2[r] = row
        for j in (0, 1):
            halves[j] = cot[:, :, 128 * j : 128 * (j + 1)].reshape(256, 128)
        left = beside(
            [
                stack([halves[j, pl.ds(2 * i + a, CH, stride=16), :] for i in range(8)])
                for a in (0, 1)
                for j in (0, 1)
            ]
        )
        out = mul3(split(left), (h3[...], l3[...]), NN)
        up2 = block_sum(out, 8, tile)
        side2 = block_sum(tile(out, 3), 8, lambda x, da: roll(x, -4 * da))
        top = inside_mask(HALO[2], tx, grid[1] - 1, False)
        ones = jnp.ones((1, 128), F32)
        up2 = clear_outside(up2, 1, ones, ty, grid[0] - 1)
        side2 = clear_outside(side2, 1, top, ty, grid[0] - 1)
        for r, row in enumerate(up2):
            u2[r] = row
        none = [jnp.zeros((CH, 128), F32)]
        up2, side2 = none + up2 + none, none + side2 + none
        left = beside(
            [stack(up2[0::2]), stack(up2[1::2]), stack(side2[0::2]) + roll(stack(side2[1::2]), 4)]
        )
        up1 = block_sum(mul3(split(left), (h2[...], l2[...]), NN), 6, tile)
        up1 = clear_outside(up1, 2, inside_mask(HALO[1], tx, grid[1] - 1, True), ty, grid[0] - 1)
        for r, row in enumerate(up1):
            u1[r] = row
        left = beside([stack(up1[0::2]), stack(up1[1::2])])
        up0 = block_sum(mul3(split(left), (h1[...], l1[...]), NN), 4, tile)
        for r, row in enumerate(up0):
            u0[r] = row

    return body


def second_kernel(grid):
    def body(got_a, got_b, g0, g1, g2, u0, u1, u2, send_a, send_b, x0, x1, s2, v0, v1, v2):
        ty, tx = places()
        lane = iota((CH, 128), 1)
        even = (tx & 1) == 0
        k = 0
        left, right, halo = [], [], []
        for j in (0, 1):
            first, second = got_a[j], got_b[j]
            right.append(jnp.where(even, first, second))
            left.append(jnp.where(even, second, first))
            halo.append(jnp.where((lane & 3) < 2, roll(left[j], -2), roll(right[j], 2)))

        def move(parts, k, offset, target, count):
            moved = roll(parts[k // 32], target - 4 * (k % 32) - offset)
            return jnp.where((lane >= target) & (lane < target + count), moved, 0.0)

        gs = []
        for level, ref in ((0, g0), (1, g1), (2, g2)):
            rows = []
            for r in range(ROWS[level]):
                side = move(halo, k, 0, HALO[level], 4)
                rows.append((ref[r], side) if level == 2 else ref[r] + side)
                k += 1
            gs.append(rows)
        us = []
        for level, ref in ((0, u0), (1, u1), (2, u2)):
            rows = []
            for r in range(ref.shape[0]):
                row = ref[r] + move(left, k, 2, BASE[level], 2)
                rows.append(row + move(right, k, 0, BASE[level] + COLS[level] - 2, 2))
                k += 1
            us.append(rows)

        inner0 = (lane >= BASE[0]) & (lane < BASE[0] + COLS[0])

        def payload(ends, ups):
            g = [[level[e] for e in ends] for level in gs]
            tiles = [row[0] for row in g[2]]
            tiles += [one + zero + two[1] for zero, one, two in zip(*g)]
            tiles.append(us[2][-ups])
            tiles += [
                jnp.where(inner0, us[0][e], us[1][e]) for e in ends
            ]
            return tiles

        low, high = payload((0, 1), 0), payload((-2, -1), 1)
        even = (ty & 1) == 0
        for j in range(len(low)):
            send_a[j] = jnp.where(even, high[j], low[j])
            send_b[j] = jnp.where(even, low[j], high[j])
        for ref, rows in ((x0, gs[0]), (x1, gs[1]), (s2, [row[1] for row in gs[2]])):
            for j, row in enumerate(rows):
                ref[j] = row
        for ref, rows, trim in ((v0, us[0], 2), (v1, us[1], 2), (v2, us[2], 1)):
            for j in range(ref.shape[0]):
                ref[j] = rows[j + trim]

    return body


def third_kernel(grid):
    def body(factor, got_a, got_b, x0, x1, g2, s2, v0, v1, v2, local, h1, l1, h2, l2, h3, l3, mix_h, mix_l, back0, back1, back2, sky, d0, d1, d2):
        ty, tx = places()
        even = (ty & 1) == 0
        above, below = [], []
        for j in range(7):
            first, second = got_a[j], got_b[j]
            above.append(jnp.where(even, second, first))
            below.append(jnp.where(even, first, second))

        def trio(rows):
            return beside([stack(rows[da : da + len(rows) - 2]) for da in (0, 1, 2)])

        field = above[2:4] + [x0[r] for r in range(2)] + below[2:4]
        out = mul3(split(trio(field)), (h1[...], l1[...]), NT)
        mixed = above[2:4] + [x1[r] for r in range(4)] + below[2:4]
        field = [tile(out[CH * i : CH * (i + 1)], a) for i in range(4) for a in (0, 1)]
        field = [f + m for f, m in zip(field, mixed)]
        mask = inside_mask(HALO[1], tx, grid[1] - 1, True)
        field = clear_outside(field, 2, mask, ty, grid[0] - 1)
        out = mul3(split(trio(field)), (h2[...], l2[...]), NT)
        mixed = above[0:2] + [g2[r] for r in range(8)] + below[0:2]
        side = above[2:4] + [s2[r] for r in range(8)] + below[2:4]
        pairs = [(out[CH * i : CH * (i + 1)], a) for i in range(6) for a in (0, 1)]
        field = [tile(o, a) + m for (o, a), m in zip(pairs, mixed)]
        side = [roll(tile(o, 2), -4 * a) + m for (o, a), m in zip(pairs, side)]
        field = clear_outside(field, 2, jnp.ones((1, 128), F32), ty, grid[0] - 1)[1:11]
        mask = inside_mask(HALO[2], tx, grid[1] - 1, False)
        side = clear_outside(side, 2, mask, ty, grid[0] - 1)[1:11]
        sides = [side[i] + roll(side[i + 1], 4) + roll(side[i + 2], 8) for i in range(8)]
        out = mul3(split(beside([trio(field), stack(sides)])), (h3[...], l3[...]), NT)
        fine = split(stack([out[:, :256], out[:, 256:]]))
        sky[...] = (mul3((mix_h[...], mix_l[...]), fine, NN) + local[...]).reshape(CH, 16, 256)

        up0 = [v0[r] + above[5 + r] + below[5 + r] for r in range(2)]
        up1 = [v1[0] + above[5], v1[1] + above[6], v1[2] + below[5], v1[3] + below[6]]
        up2 = [v2[0] + above[4]] + [v2[r] for r in range(1, 7)] + [v2[7] + below[4]]
        up1 = factor_rows(up1, factor, 1, True)
        up2 = factor_rows(up2, factor, 2, True)
        for ref, rows, back, level in ((d0, up0, back0, 0), (d1, up1, back1, 1), (d2, up2, back2, 2)):
            out = mul(back[...], stack(rows))
            cols = COLS[level]
            if BASE[level]:
                out = roll(out, -BASE[level])
            out = out.reshape(CH, ROWS[level], 128)
            ref[...] = out[:, :, :cols] if cols < 128 else out

    return body


def one_hot(test):
    return jnp.where(test, 1.0, 0.0)


def local_body(factor, mixing, cot, e3, local, grad, mix_h, mix_l, back0, back1, back2):
    f = mixing[...]
    column = one_hot(iota((256, CH), 0) // CH == iota((256, CH), 1))
    spread = mul(column, f)
    same = (iota((256, 256), 0) & 15) == (iota((256, 256), 1) & 15)

    def factored(ref, transposed):
        halves = [
            factor_tile(ref[:, :, 128 * h : 128 * (h + 1)].reshape(32, 8, 128), factor, transposed).reshape(256, 128)
            for h in (0, 1)
        ]
        return split(beside(halves))

    side = split(jnp.where(same, mul_t(column, spread), 0.0))
    grad[...] = mul3(side, factored(cot, True), NN).reshape(CH, 16, 256)
    side = split(jnp.where(same, mul_t(spread, column), 0.0))
    local[...] = mul3(side, factored(e3, False), NN)
    tiled = one_hot((iota((256, CH), 0) & 15) == iota((256, CH), 1))
    col = iota((256, 256), 1)
    there = (iota((256, 256), 0) & 15) == 2 * ((col & 127) >> 4) + (col >> 7)
    mix_h[...], mix_l[...] = split(jnp.where(there, mul_t(spread, tiled), 0.0))
    for ref, rows in ((back0, 2), (back1, 4), (back2, 8)):
        n = CH * rows
        full = mul_t(one_hot(iota((n, CH), 0) // rows == iota((n, CH), 1)), stack([f] * rows))
        ref[...] = jnp.where(iota((n, n), 0) % rows == iota((n, n), 1) // CH, full, 0.0)


def swaps(count, first):
    pairs = []
    for i in range(first, count - 1, 2):
        pairs += [(i, i + 1), (i + 1, i)]
    return pairs


def shaped(*shape, dtype=F32):
    return jax.ShapeDtypeStruct(shape, dtype)


SMEM = pl.BlockSpec(memory_space=pltpu.SMEM)
VMEM = pl.BlockSpec(memory_space=pltpu.VMEM)
HBM = pl.BlockSpec(memory_space=pltpu.HBM)


def call(body, specs, outs, args, scratch=(), limit=VMEM_LIMIT):
    return pl.pallas_call(
        body,
        out_shape=outs,
        in_specs=specs,
        out_specs=[VMEM] * len(outs),
        scratch_shapes=list(scratch),
        compiler_params=pltpu.CompilerParams(vmem_limit_bytes=limit),
    )(*args)


def device_body(grid):
    def on_device(e0, e1, e2, e3, weights, factor, mixing, cot):
        rows = [shaped(2, CH, 128), shaped(4, CH, 128), shaped(8, CH, 128)]
        ups = [shaped(6, CH, 128), shaped(8, CH, 128), shaped(10, CH, 128)]
        (send,) = call(
            first_kernel(grid),
            [HBM] * 6,
            [shaped(2, CH, 128)],
            (weights, factor, cot, e0, e1, e2),
            [
                pltpu.SMEM((3, 4, 9), F32),
                pltpu.SMEM((3, 4, 4), F32),
                pltpu.VMEM((CH, 16, 256), F32),
                pltpu.VMEM((CH, 2, 32), F32),
                pltpu.VMEM((CH, 4, 64), F32),
                pltpu.VMEM((CH, 8, 128), F32),
                pltpu.VMEM((256, 128), F32),
                pltpu.SemaphoreType.DMA((6,)),
            ],
            60 * 1024 * 1024,
        )
        got_a = lax.ppermute(send, "tx", swaps(grid[1], 0))
        got_b = lax.ppermute(send, "tx", swaps(grid[1], 1))
        sizes = [(256, 384), (384, 384), (512, 512)]
        inner = call(
            inner_kernel(grid),
            [SMEM] * 2 + [VMEM] * 4,
            rows + ups + [shaped(*size, dtype=BF16) for size in sizes for _ in (0, 1)],
            (weights, factor, cot, e0, e1, e2),
            [pltpu.VMEM((2, 256, 128), F32)],
        )
        matrices = inner[6:]
        second = call(
            second_kernel(grid),
            [VMEM] * 8,
            [shaped(7, CH, 128)] * 2 + rows + rows,
            (got_a, got_b, *inner[:6]),
        )
        local, grad3, *mixes = call(
            local_body,
            [SMEM] + [VMEM] * 3,
            [shaped(256, 256), shaped(CH, 16, 256)]
            + [shaped(256, 256, dtype=BF16)] * 2
            + [shaped(32, 32), shaped(64, 64), shaped(128, 128)],
            (factor, mixing, cot, e3),
        )
        got_a = lax.ppermute(second[0], "ty", swaps(grid[0], 0))
        got_b = lax.ppermute(second[1], "ty", swaps(grid[0], 1))
        x0, x1, s2, v0, v1, v2 = second[2:]
        sky, grad0, grad1, grad2 = call(
            third_kernel(grid),
            [SMEM] + [VMEM] * 21,
            [shaped(CH, 16, 256), shaped(CH, 2, 32), shaped(CH, 4, 64), shaped(CH, 8, 128)],
            (factor, got_a, got_b, x0, x1, inner[2], s2, v0, v1, v2, local, *matrices, *mixes),
        )
        return (sky, grad0, grad1, grad2, grad3)

    return on_device


def solution(mesh):
    tiles = P(None, "ty", "tx")
    return jax.shard_map(
        device_body((mesh.shape["ty"], mesh.shape["tx"])),
        mesh=mesh,
        in_specs=(tiles, tiles, tiles, tiles, P(), P(), P(), tiles),
        out_specs=(tiles,) * 5,
        check_vma=False,
    )
```

time: 39.6 us -> 30.2 us (0.76)
  the two profiles are of different devices: /device:TPU:225 before, /device:TPU:233 now
where the time goes in v2:
time: 30.2 us; the launch traced here: 30 us
  starting transfers between devices  16.2 us (54%)
  Pallas kernels  12.5 us (41%)
  between operations  0.82 us (3%)
  waiting for transfers between devices  0.38 us (1%)
    pallas_call x5, Pallas kernels, call(): pl.pallas_call(body, out_shape=outs, in_specs=specs, out_specs=[VMEM] * l...  12.5 us
    ppermute x1, starting transfers between devices, on_device(): got_b = lax.ppermute(send, 'tx', swaps(grid[1], 1))  5.17 us
    ppermute x1, starting transfers between devices, on_device(): got_b = lax.ppermute(second[1], 'ty', swaps(grid[0], 1))  5.11 us
    ppermute x1, starting transfers between devices, on_device(): got_a = lax.ppermute(second[0], 'ty', swaps(grid[0], 0))  4.01 us
    ppermute x1, starting transfers between devices, on_device(): got_a = lax.ppermute(send, 'tx', swaps(grid[1], 0))  1.92 us
  transfers between devices with their start and end apart: 4, of which 1 were waited for; matrix products, arithmetic and copies ran while one was open for 0% of the time, Pallas kernels for 18%

profile of v2, /device:TPU:233, one launch (start us, length us, event | category | flops | bytes accessed | tf_op | source)
XLA Modules:
  0.0 30.0 jit_solution(15789635153989643716)
XLA Ops:
  0.6 0.0 copy-start.4
  0.6 0.0 copy-start
  0.7 0.0 copy-start.6
  0.7 0.0 copy-start.2
  0.7 0.0 copy-start.3
  0.7 0.0 copy-start.5
  0.7 3.7 %shard_map.119 = f32[2,16,128]{2,1,0:T(8,128)} custom-call(f32[3,4,9]{2,1,0:T(4,128)} %weights.1, f32[3,4,4]{2,1,0:T(4,128)} %factor.5, f32[16,16,256]{2,1,0:T(8,128)} %cot.3, f32[16,2,32]{2,1,0:T(2,128)} %e0.1, f32[16,4,64]{2,1,0:T(4,128)} %e1.1, f32[16,8,128]{2,1,0:T(8,128)} %e2.1), custom_call_target="tpu_custom_call" | custom-call | tf_op jit(solution)/shard_map/pallas_call | solution.py:532
  4.4 5.2 %collective-permute-start.1 = (f32[2,16,128]{2,1,0:T(8,128)}, f32[2,16,128]{2,1,0:T(8,128)S(1)}, u32[]{:S(2)}, u32[]{:S(2)}) collective-permute-start(f32[2,16,128]{2,1,0:T(8,128)} %shard_map.119), channel_id=1, source_target_pairs={{1,2},{2,1},{3,4},{4,3},{5,6},{6,5},{7,8},{8,7},{9,10},{10,9},{11,... | collective-permute-start | bytes 49160 | tf_op jit(solution)/shard_map/ppermute | solution.py:564
  9.6 1.9 %collective-permute-start = (f32[2,16,128]{2,1,0:T(8,128)}, f32[2,16,128]{2,1,0:T(8,128)S(1)}, u32[]{:S(2)}, u32[]{:S(2)}) collective-permute-start(f32[2,16,128]{2,1,0:T(8,128)} %shard_map.119), channel_id=1, source_target_pairs={{0,1},{1,0},{2,3},{3,2},{4,5},{5,4},{6,7},{7,6},{8,9},{9,8},{10,11... | collective-permute-start | bytes 49160 | tf_op jit(solution)/shard_map/ppermute | solution.py:563
  11.5 0.0 copy-done.4
  11.5 0.0 copy-done
  11.5 0.0 copy-done.6
  11.5 0.0 copy-done.2
  11.5 0.0 copy-done.3
  11.6 0.0 copy-done.5
  11.6 2.3 %shard_map.120 = (f32[2,16,128]{2,1,0:T(8,128)S(1)}, f32[4,16,128]{2,1,0:T(8,128)S(1)}, f32[8,16,128]{2,1,0:T(8,128)S(1)}, f32[6,16,128]{2,1,0:T(8,128)S(1)}, f3...) custom-call(f32[3,4,9]{2,1,0:T(4,128)S(1)} %copy-done.6, ...), custom_call_target="tpu_custom_call" | custom-call | tf_op jit(solution)/shard_map/pallas_call | solution.py:532
  13.9 0.0 copy-start.1
  13.9 0.0 collective-permute-done.1.got_b
  13.9 0.4 %collective-permute-done.got_a = f32[2,16,128]{2,1,0:T(8,128)S(1)} collective-permute-done((f32[2,16,128]{2,1,0:T(8,128)}, f32[2,16,128]{2,1,0:T(8,128)S(1)}, u32[]{:S(2)}, u32[]{:S(2)}) %collective-permute-start) | collective-permute-done | bytes 16416 | tf_op jit(solution)/shard_map/ppermute | solution.py:563
  14.3 0.0 copy-start.7
  14.3 0.2 shard_map.121
  14.5 4.0 %collective-permute-start.2 = (f32[7,16,128]{2,1,0:T(8,128)S(1)}, f32[7,16,128]{2,1,0:T(8,128)S(1)}, u32[]{:S(2)}, u32[]{:S(2)}) collective-permute-start(f32[7,16,128]{2,1,0:T(8,128)S(1)} %get-tuple-element.42), channel_id=1, source_target_pairs={{0,32},{32,0},{64,96},{96,64},{128,160},{160,128},{192,224},{224,1... | collective-permute-start | bytes 172040 | tf_op jit(solution)/shard_map/ppermute | solution.py:588
  18.5 5.1 %collective-permute-start.3 = (f32[7,16,128]{2,1,0:T(8,128)S(1)}, f32[7,16,128]{2,1,0:T(8,128)S(1)}, u32[]{:S(2)}, u32[]{:S(2)}) collective-permute-start(f32[7,16,128]{2,1,0:T(8,128)S(1)} %get-tuple-element.43), channel_id=1, source_target_pairs={{32,64},{64,32},{96,128},{128,96},{160,192},{192,160},{224,256},{2... | collective-permute-start | bytes 172040 | tf_op jit(solution)/shard_map/ppermute | solution.py:589
  23.6 0.0 copy-done.1
  23.6 0.0 copy-done.7
  23.7 3.1 %shard_map.122 = (f32[256,256]{1,0:T(8,128)S(1)}, f32[16,16,256]{2,1,0:T(8,128)}, bf16[256,256]{1,0:T(8,128)(2,1)S(1)}, bf16[256,256]{1,0:T(8,128)(2,1)S(1)}, f3...) custom-call(f32[3,4,4]{2,1,0:T(4,128)S(1)} %copy-done.4, f32[16,16]{1,0:T(8,128)S(1)} %copy-done.7, ...), custom_call_target="tpu_custom_call" | custom-call | tf_op jit(solution)/shard_map/pallas_call | solution.py:532
  26.8 0.0 collective-permute-done.2.got_a
  26.8 0.0 collective-permute-done.3.got_b
  26.8 3.2 %shard_map.123 = (f32[16,16,256]{2,1,0:T(8,128)}, f32[16,2,32]{2,1,0:T(2,128)}, f32[16,4,64]{2,1,0:T(4,128)}, f32[16,8,128]{2,1,0:T(8,128)}) custom-call(f32[3,4,4]{2,1,0:T(4,128)S(1)} %copy-done.4, f32[7,16,128]{2,1,0:T(8,128)S(1)} %collective-permute-done.2.got_a, f32[7,16,128]{2,1,0:T(8,128)S(1)} %collective-permute-done.3.got_b, ...), custom_call_target="tpu_custom_call" | custom-call | tf_op jit(solution)/shard_map/pallas_call | solution.py:532
Async XLA Ops:
  0.6 10.9 %copy-start.4 = (f32[3,4,4]{2,1,0:T(4,128)S(1)}, f32[3,4,4]{2,1,0:T(4,128)}, u32[]{:S(2)}) copy-start(f32[3,4,4]{2,1,0:T(4,128)} %factor.5) | copy-start | bytes 580
  0.6 10.9 %copy-start = (f32[16,16,256]{2,1,0:T(8,128)S(1)}, f32[16,16,256]{2,1,0:T(8,128)}, u32[]{:S(2)}) copy-start(f32[16,16,256]{2,1,0:T(8,128)} %cot.3) | copy-start | bytes 786436
  0.7 10.9 %copy-start.6 = (f32[3,4,9]{2,1,0:T(4,128)S(1)}, f32[3,4,9]{2,1,0:T(4,128)}, u32[]{:S(2)}) copy-start(f32[3,4,9]{2,1,0:T(4,128)} %weights.1) | copy-start | bytes 1300
  0.7 10.9 %copy-start.2 = (f32[16,8,128]{2,1,0:T(8,128)S(1)}, f32[16,8,128]{2,1,0:T(8,128)}, u32[]{:S(2)}) copy-start(f32[16,8,128]{2,1,0:T(8,128)} %e2.1) | copy-start | bytes 196612
  0.7 10.9 %copy-start.3 = (f32[16,4,64]{2,1,0:T(4,128)S(1)}, f32[16,4,64]{2,1,0:T(4,128)}, u32[]{:S(2)}) copy-start(f32[16,4,64]{2,1,0:T(4,128)} %e1.1) | copy-start | bytes 49156
  0.7 10.9 %copy-start.5 = (f32[16,2,32]{2,1,0:T(2,128)S(1)}, f32[16,2,32]{2,1,0:T(2,128)}, u32[]{:S(2)}) copy-start(f32[16,2,32]{2,1,0:T(2,128)} %e0.1) | copy-start | bytes 12292
  4.4 9.5 %collective-permute-start.1 = (f32[2,16,128]{2,1,0:T(8,128)}, f32[2,16,128]{2,1,0:T(8,128)S(1)}, u32[]{:S(2)}, u32[]{:S(2)}) collective-permute-start(f32[2,16,128]{2,1,0:T(8,128)} %shard_map.119), channel_id=1, source_target_pairs={{1,2},{2,1},{3,4},{4,3},{5,6},{6,5},{7,8},{8,7},{9,10},{10,9},{11,... | collective-permute-start | bytes 49160 | tf_op jit(solution)/shard_map/ppermute | solution.py:564
  9.6 4.7 %collective-permute-start = (f32[2,16,128]{2,1,0:T(8,128)}, f32[2,16,128]{2,1,0:T(8,128)S(1)}, u32[]{:S(2)}, u32[]{:S(2)}) collective-permute-start(f32[2,16,128]{2,1,0:T(8,128)} %shard_map.119), channel_id=1, source_target_pairs={{0,1},{1,0},{2,3},{3,2},{4,5},{5,4},{6,7},{7,6},{8,9},{9,8},{10,11... | collective-permute-start | bytes 49160 | tf_op jit(solution)/shard_map/ppermute | solution.py:563
  13.9 9.8 %copy-start.1 = (f32[16,16,256]{2,1,0:T(8,128)S(1)}, f32[16,16,256]{2,1,0:T(8,128)}, u32[]{:S(2)}) copy-start(f32[16,16,256]{2,1,0:T(8,128)} %e3.1) | copy-start | bytes 786436
  14.3 9.4 %copy-start.7 = (f32[16,16]{1,0:T(8,128)S(1)}, f32[16,16]{1,0:T(8,128)}, u32[]{:S(2)}) copy-start(f32[16,16]{1,0:T(8,128)} %mixing.1) | copy-start | bytes 3076
  14.5 12.3 %collective-permute-start.2 = (f32[7,16,128]{2,1,0:T(8,128)S(1)}, f32[7,16,128]{2,1,0:T(8,128)S(1)}, u32[]{:S(2)}, u32[]{:S(2)}) collective-permute-start(f32[7,16,128]{2,1,0:T(8,128)S(1)} %get-tuple-element.42), channel_id=1, source_target_pairs={{0,32},{32,0},{64,96},{96,64},{128,160},{160,128},{192,224},{224,1... | collective-permute-start | bytes 172040 | tf_op jit(solution)/shard_map/ppermute | solution.py:588
  18.5 8.3 %collective-permute-start.3 = (f32[7,16,128]{2,1,0:T(8,128)S(1)}, f32[7,16,128]{2,1,0:T(8,128)S(1)}, u32[]{:S(2)}, u32[]{:S(2)}) collective-permute-start(f32[7,16,128]{2,1,0:T(8,128)S(1)} %get-tuple-element.43), channel_id=1, source_target_pairs={{32,64},{64,32},{96,128},{128,96},{160,192},{192,160},{224,256},{2... | collective-permute-start | bytes 172040 | tf_op jit(solution)/shard_map/ppermute | solution.py:589

commit v3 on v2

--- a/solution.py
+++ b/solution.py
@@ -96,31 +96,46 @@
 FAR, NEAR = -4096, 4096
 
 
+def zeros(count):
+    return jnp.zeros((count, 128), F32)
+
+
 def matrix_1(weights):
-    fine, coarse = fine_index(128), lane_index(128)
-    fine, coarse = both_col(fine, 1, FAR), both_col(coarse, 0, NEAR)
-    return [[refine_weight(weights, 1, fine, coarse, a, da) for da in (0, 1, 2)] for a in (0, 1)]
+    group = iota((9, 8, 128), 0)
+    fine = jnp.where(group < 8, group, HALO[1] // 8) * 8 + iota((9, 8, 128), 1)
+    fine, coarse = both_col(fine, 1, FAR), both_col(lane_index(72), 0, NEAR)
+    rows = []
+    for a in (0, 1):
+        row = []
+        for da in (0, 1, 2):
+            block = refine_weight(weights, 1, fine, coarse, a, da)
+            row.append(stack([block[:64], zeros(32), block[64:], zeros(24)]))
+        rows.append(row)
+    return rows
 
 
 def matrix_2(weights):
     index, coarse = fine_index(128), both_col(lane_index(128), 1, NEAR)
-    inner = interior_col(index, 2, FAR)
-    rows = [[refine_weight(weights, 2, inner, coarse, a, da) for da in (0, 1, 2)] for a in (0, 1)]
+    rows = [[refine_weight(weights, 2, index, coarse, a, da) for da in (0, 1, 2)] for a in (0, 1)]
+    index, coarse = HALO[2] + iota((1, 8, 128), 1), coarse[:1]
     halos = [halo_col(index, 2, HALO[2] + 4 * a, FAR) for a in (0, 1)]
-    rows.append(
-        [sum(refine_weight(weights, 2, halos[a], coarse, a, da) for a in (0, 1)) for da in (0, 1, 2)]
-    )
+    row = []
+    for da in (0, 1, 2):
+        block = sum(refine_weight(weights, 2, halos[a], coarse, a, da) for a in (0, 1))
+        row.append(stack([zeros(HALO[2]), block, zeros(120 - HALO[2])]))
+    rows.append(row)
     return rows
 
 
 def matrix_3(weights):
     index, lane = fine_index(256), lane_index(256)
-    inner = interior_col(lane, 2, NEAR)
-    halos = [halo_col(lane, 2, HALO[2] + 4 * da, NEAR) for da in (0, 1, 2)]
+    ends = iota((2, 8, 128), 0) * 248 + iota((2, 8, 128), 1)
+    halos = [halo_col(lane_index(16), 2, HALO[2] + 4 * da, NEAR) for da in (0, 1, 2)]
     rows = []
     for a in (0, 1):
-        row = [refine_weight(weights, 3, index, inner, a, da) for da in (0, 1, 2)]
-        row.append(sum(refine_weight(weights, 3, index, halos[da], a, da) for da in (0, 1, 2)))
+        row = [refine_weight(weights, 3, index, lane, a, da) for da in (0, 1, 2)]
+        block = sum(refine_weight(weights, 3, ends, halos[da], a, da) for da in (0, 1, 2))
+        row.append(stack([block[:8], zeros(240), block[8:]]))
         rows.append(row)
     return rows
 
@@ -258,19 +273,18 @@
     )
 
 
-def edge_pull(rows, weights, level, width):
-    blocks = len(rows) // 2
+def edge_matrix(weights, level, width):
     fine = edge_col(fine_index(width), level, FAR)
     coarse = edge_col(lane_index(width), level - 1, NEAR)
-    parts = []
-    for da in (0, 1, 2):
-        total = None
-        for a in (0, 1):
-            left = stack([rows[2 * i + a] for i in range(blocks)])[:, :width]
-            term = mul(left, refine_weight(weights, level, fine, coarse, a, da))
-            total = term if total is None else total + term
-        parts.append(total)
-    return block_sum(beside(parts), blocks, tile)
+    return split(
+        stack([beside([refine_weight(weights, level, fine, coarse, a, da) for da in (0, 1, 2)]) for a in (0, 1)])
+    )
+
+
+def edge_pull(rows, matrix, width):
+    even, odd = stack(rows[0::2]), stack(rows[1::2])
+    left = jnp.where(iota(even.shape, 1) < width, even, roll(odd, width))[:, : 2 * width]
+    return block_sum(mul3(split(left), matrix, NN), len(rows) // 2, tile)
 
 
 def widen(x):
@@ -291,27 +305,27 @@
             copy.start()
         ty, tx = places()
         lane = iota((CH, 128), 1)
-        for copy in copies[2:]:
+        for copy in copies[1:]:
             copy.wait()
-
-        def edges(row, level):
+        edges = [edge_matrix(weights, level, (0, 8, 16, 32)[level]) for level in (1, 2, 3)]
+
+        def ends(row, level):
             return jnp.where(lane < 2, row, roll(row, 4 - COLS[level]))
 
-        pieces = [edges(widen(e0[:, r, :]), 0) for r in range(2)]
-        pieces += factor_rows([edges(widen(e1[:, r, :]), 1) for r in range(4)], factor, 1, False)
-        pieces += factor_rows([edges(e2[:, r, :], 2) for r in range(8)], factor, 2, False)
-        for copy in copies[:2]:
-            copy.wait()
+        pieces = [ends(widen(e0[:, r, :]), 0) for r in range(2)]
+        pieces += factor_rows([ends(widen(e1[:, r, :]), 1) for r in range(4)], factor, 1, False)
+        pieces += factor_rows([ends(e2[:, r, :], 2) for r in range(8)], factor, 2, False)
+        copies[0].wait()
         low = cot[:, :, :128].reshape(256, 128)
         high = cot[:, :, 128:].reshape(256, 128)
         edge[...] = jnp.where(iota((256, 128), 1) < 16, low, roll(high, 32))
         rows = [edge[pl.ds(r, CH, stride=16), :] for r in range(16)]
         mask = inside_mask(0, tx, grid[1] - 1, True)
-        up2 = clear_outside(edge_pull(rows, weights, 3, 32), 1, mask, ty, grid[0] - 1)
+        up2 = clear_outside(edge_pull(rows, edges[2], 32), 1, mask, ty, grid[0] - 1)
         none = jnp.zeros((CH, 128), F32)
-        up1 = edge_pull([none] + up2 + [none], weights, 2, 16)
+        up1 = edge_pull([none] + up2 + [none], edges[1], 16)
         up1 = clear_outside(up1, 2, mask, ty, grid[0] - 1)
-        up0 = edge_pull(up1, weights, 1, 8)
+        up0 = edge_pull(up1, edges[0], 8)
         pieces += up0 + up1 + up2
         totals = [none, none]
         for k, piece in enumerate(pieces):
@@ -482,14 +496,17 @@
 
 
 def one_hot(test):
-    return jnp.where(test, 1.0, 0.0)
-
-
-def local_body(factor, mixing, cot, e3, local, grad, mix_h, mix_l, back0, back1, back2):
-    f = mixing[...]
+    return jnp.where(test, 1.0, 0.0).astype(BF16)
+
+
+def local_body(factor, mixing, cot, e3, local, grad_out, mix_h, mix_l, back0, back1, back2, grad, sem):
+    parts = split(mixing[...])
     column = one_hot(iota((256, CH), 0) // CH == iota((256, CH), 1))
-    spread = mul(column, f)
+    spread = [dot(column, f, NN).astype(BF16) for f in parts]
     same = (iota((256, 256), 0) & 15) == (iota((256, 256), 1) & 15)
+
+    def select(where, pairs):
+        return [jnp.where(where, dot(x, y, NT), 0.0).astype(BF16) for x, y in pairs]
 
     def factored(ref, transposed):
         halves = [
@@ -498,18 +515,22 @@
         ]
         return split(beside(halves))
 
-    side = split(jnp.where(same, mul_t(column, spread), 0.0))
+    side = select(same, [(column, f) for f in spread])
     grad[...] = mul3(side, factored(cot, True), NN).reshape(CH, 16, 256)
-    side = split(jnp.where(same, mul_t(spread, column), 0.0))
+    copy = pltpu.make_async_copy(grad, grad_out, sem)
+    copy.start()
+    side = select(same, [(f, column) for f in spread])
     local[...] = mul3(side, factored(e3, False), NN)
     tiled = one_hot((iota((256, CH), 0) & 15) == iota((256, CH), 1))
     col = iota((256, 256), 1)
     there = (iota((256, 256), 0) & 15) == 2 * ((col & 127) >> 4) + (col >> 7)
-    mix_h[...], mix_l[...] = split(jnp.where(there, mul_t(spread, tiled), 0.0))
+    mix_h[...], mix_l[...] = select(there, [(f, tiled) for f in spread])
     for ref, rows in ((back0, 2), (back1, 4), (back2, 8)):
         n = CH * rows
-        full = mul_t(one_hot(iota((n, CH), 0) // rows == iota((n, CH), 1)), stack([f] * rows))
-        ref[...] = jnp.where(iota((n, n), 0) % rows == iota((n, n), 1) // CH, full, 0.0)
+        one = one_hot(iota((n, CH), 0) // rows == iota((n, CH), 1))
+        full = [dot(one, stack([f] * rows), NT) for f in parts]
+        ref[...] = jnp.where(iota((n, n), 0) % rows == iota((n, n), 1) // CH, full[0] + full[1], 0.0)
+    copy.wait()
 
 
 def swaps(count, first):
@@ -528,12 +549,12 @@
 HBM = pl.BlockSpec(memory_space=pltpu.HBM)
 
 
-def call(body, specs, outs, args, scratch=(), limit=VMEM_LIMIT):
+def call(body, specs, outs, args, scratch=(), limit=VMEM_LIMIT, into=None):
     return pl.pallas_call(
         body,
         out_shape=outs,
         in_specs=specs,
-        out_specs=[VMEM] * len(outs),
+        out_specs=[HBM if k == into else VMEM for k in range(len(outs))],
         scratch_shapes=list(scratch),
         compiler_params=pltpu.CompilerParams(vmem_limit_bytes=limit),
     )(*args)
@@ -584,6 +605,8 @@
             + [shaped(256, 256, dtype=BF16)] * 2
             + [shaped(32, 32), shaped(64, 64), shaped(128, 128)],
             (factor, mixing, cot, e3),
+            [pltpu.VMEM((CH, 16, 256), F32), pltpu.SemaphoreType.DMA],
+            into=1,
         )
         got_a = lax.ppermute(second[0], "ty", swaps(grid[0], 0))
         got_b = lax.ppermute(second[1], "ty", swaps(grid[0], 1))

time: 30.2 us -> 28.4 us (0.940)
  the two profiles are of different devices: /device:TPU:233 before, /device:TPU:249 now
where the time goes in v3:
time: 28.4 us; the launch traced here: 28.2 us
  starting transfers between devices  16.2 us (57%)
  Pallas kernels  10.5 us (37%)
  between operations  0.84 us (3%)
  waiting for transfers between devices  0.55 us (2%)
    pallas_call x5, Pallas kernels, call(): pl.pallas_call(body, out_shape=outs, in_specs=specs, out_specs=[HBM if k...  10.5 us
    ppermute x1, starting transfers between devices, on_device(): got_b = lax.ppermute(send, 'tx', swaps(grid[1], 1))  5.16 us
    ppermute x1, starting transfers between devices, on_device(): got_b = lax.ppermute(second[1], 'ty', swaps(grid[0], 1))  5.11 us
    ppermute x1, starting transfers between devices, on_device(): got_a = lax.ppermute(second[0], 'ty', swaps(grid[0], 0))  4.02 us
    ppermute x1, starting transfers between devices, on_device(): got_a = lax.ppermute(send, 'tx', swaps(grid[1], 0))  1.92 us
  transfers between devices with their start and end apart: 4, of which 1 were waited for; matrix products, arithmetic and copies ran while one was open for 0% of the time, Pallas kernels for 15%

profile of v3, /device:TPU:249, one launch (start us, length us, event | category | flops | bytes accessed | tf_op | source)
XLA Modules:
  0.0 28.2 jit_solution(3230275682022549038)
XLA Ops:
  0.6 0.0 copy-start.4
  0.6 0.0 copy-start
  0.7 0.0 copy-start.6
  0.7 0.0 copy-start.2
  0.7 0.0 copy-start.3
  0.7 0.0 copy-start.5
  0.7 2.9 %shard_map.119 = f32[2,16,128]{2,1,0:T(8,128)} custom-call(f32[3,4,9]{2,1,0:T(4,128)} %weights.1, f32[3,4,4]{2,1,0:T(4,128)} %factor.5, f32[16,16,256]{2,1,0:T(8,128)} %cot.3, f32[16,2,32]{2,1,0:T(2,128)} %e0.1, f32[16,4,64]{2,1,0:T(4,128)} %e1.1, f32[16,8,128]{2,1,0:T(8,128)} %e2.1), custom_call_target="tpu_custom_call" | custom-call | tf_op jit(solution)/shard_map/pallas_call | solution.py:553
  3.6 5.2 %collective-permute-start.1 = (f32[2,16,128]{2,1,0:T(8,128)}, f32[2,16,128]{2,1,0:T(8,128)S(1)}, u32[]{:S(2)}, u32[]{:S(2)}) collective-permute-start(f32[2,16,128]{2,1,0:T(8,128)} %shard_map.119), channel_id=1, source_target_pairs={{1,2},{2,1},{3,4},{4,3},{5,6},{6,5},{7,8},{8,7},{9,10},{10,9},{11,... | collective-permute-start | bytes 49160 | tf_op jit(solution)/shard_map/ppermute | solution.py:585
  8.8 1.9 %collective-permute-start = (f32[2,16,128]{2,1,0:T(8,128)}, f32[2,16,128]{2,1,0:T(8,128)S(1)}, u32[]{:S(2)}, u32[]{:S(2)}) collective-permute-start(f32[2,16,128]{2,1,0:T(8,128)} %shard_map.119), channel_id=1, source_target_pairs={{0,1},{1,0},{2,3},{3,2},{4,5},{5,4},{6,7},{7,6},{8,9},{9,8},{10,11... | collective-permute-start | bytes 49160 | tf_op jit(solution)/shard_map/ppermute | solution.py:584
  10.8 0.0 copy-done.4
  10.8 0.0 copy-done
  10.8 0.0 copy-done.6
  10.8 0.0 copy-done.2
  10.8 0.0 copy-done.3
  10.8 0.0 copy-done.5
  10.8 2.1 %shard_map.120 = (f32[2,16,128]{2,1,0:T(8,128)S(1)}, f32[4,16,128]{2,1,0:T(8,128)S(1)}, f32[8,16,128]{2,1,0:T(8,128)S(1)}, f32[6,16,128]{2,1,0:T(8,128)S(1)}, f3...) custom-call(f32[3,4,9]{2,1,0:T(4,128)S(1)} %copy-done.6, ...), custom_call_target="tpu_custom_call" | custom-call | tf_op jit(solution)/shard_map/pallas_call | solution.py:553
  13.0 0.0 copy-start.1
  13.0 0.0 collective-permute-done.1.got_b
  13.0 0.5 %collective-permute-done.got_a = f32[2,16,128]{2,1,0:T(8,128)S(1)} collective-permute-done((f32[2,16,128]{2,1,0:T(8,128)}, f32[2,16,128]{2,1,0:T(8,128)S(1)}, u32[]{:S(2)}, u32[]{:S(2)}) %collective-permute-start) | collective-permute-done | bytes 16416 | tf_op jit(solution)/shard_map/ppermute | solution.py:584
  13.5 0.0 copy-start.7
  13.5 0.2 shard_map.121
  13.7 4.0 %collective-permute-start.2 = (f32[7,16,128]{2,1,0:T(8,128)S(1)}, f32[7,16,128]{2,1,0:T(8,128)S(1)}, u32[]{:S(2)}, u32[]{:S(2)}) collective-permute-start(f32[7,16,128]{2,1,0:T(8,128)S(1)} %get-tuple-element.42), channel_id=1, source_target_pairs={{0,32},{32,0},{64,96},{96,64},{128,160},{160,128},{192,224},{224,1... | collective-permute-start | bytes 172040 | tf_op jit(solution)/shard_map/ppermute | solution.py:611
  17.8 5.1 %collective-permute-start.3 = (f32[7,16,128]{2,1,0:T(8,128)S(1)}, f32[7,16,128]{2,1,0:T(8,128)S(1)}, u32[]{:S(2)}, u32[]{:S(2)}) collective-permute-start(f32[7,16,128]{2,1,0:T(8,128)S(1)} %get-tuple-element.43), channel_id=1, source_target_pairs={{32,64},{64,32},{96,128},{128,96},{160,192},{192,160},{224,256},{2... | collective-permute-start | bytes 172040 | tf_op jit(solution)/shard_map/ppermute | solution.py:612
  22.9 0.0 copy-done.1
  22.9 0.0 copy-done.7
  22.9 2.0 %shard_map.122 = (f32[256,256]{1,0:T(8,128)S(1)}, f32[16,16,256]{2,1,0:T(8,128)}, bf16[256,256]{1,0:T(8,128)(2,1)S(1)}, bf16[256,256]{1,0:T(8,128)(2,1)S(1)}, f3...) custom-call(f32[3,4,4]{2,1,0:T(4,128)S(1)} %copy-done.4, f32[16,16]{1,0:T(8,128)S(1)} %copy-done.7, ...), custom_call_target="tpu_custom_call" | custom-call | tf_op jit(solution)/shard_map/pallas_call | solution.py:553
  24.9 0.0 collective-permute-done.2.got_a
  24.9 0.0 collective-permute-done.3.got_b
  25.0 3.2 %shard_map.123 = (f32[16,16,256]{2,1,0:T(8,128)}, f32[16,2,32]{2,1,0:T(2,128)}, f32[16,4,64]{2,1,0:T(4,128)}, f32[16,8,128]{2,1,0:T(8,128)}) custom-call(f32[3,4,4]{2,1,0:T(4,128)S(1)} %copy-done.4, f32[7,16,128]{2,1,0:T(8,128)S(1)} %collective-permute-done.2.got_a, f32[7,16,128]{2,1,0:T(8,128)S(1)} %collective-permute-done.3.got_b, ...), custom_call_target="tpu_custom_call" | custom-call | tf_op jit(solution)/shard_map/pallas_call | solution.py:553
Async XLA Ops:
  0.6 10.1 %copy-start.4 = (f32[3,4,4]{2,1,0:T(4,128)S(1)}, f32[3,4,4]{2,1,0:T(4,128)}, u32[]{:S(2)}) copy-start(f32[3,4,4]{2,1,0:T(4,128)} %factor.5) | copy-start | bytes 580
  0.6 10.1 %copy-start = (f32[16,16,256]{2,1,0:T(8,128)S(1)}, f32[16,16,256]{2,1,0:T(8,128)}, u32[]{:S(2)}) copy-start(f32[16,16,256]{2,1,0:T(8,128)} %cot.3) | copy-start | bytes 786436
  0.7 10.1 %copy-start.6 = (f32[3,4,9]{2,1,0:T(4,128)S(1)}, f32[3,4,9]{2,1,0:T(4,128)}, u32[]{:S(2)}) copy-start(f32[3,4,9]{2,1,0:T(4,128)} %weights.1) | copy-start | bytes 1300
  0.7 10.1 %copy-start.2 = (f32[16,8,128]{2,1,0:T(8,128)S(1)}, f32[16,8,128]{2,1,0:T(8,128)}, u32[]{:S(2)}) copy-start(f32[16,8,128]{2,1,0:T(8,128)} %e2.1) | copy-start | bytes 196612
  0.7 10.1 %copy-start.3 = (f32[16,4,64]{2,1,0:T(4,128)S(1)}, f32[16,4,64]{2,1,0:T(4,128)}, u32[]{:S(2)}) copy-start(f32[16,4,64]{2,1,0:T(4,128)} %e1.1) | copy-start | bytes 49156
  0.7 10.1 %copy-start.5 = (f32[16,2,32]{2,1,0:T(2,128)S(1)}, f32[16,2,32]{2,1,0:T(2,128)}, u32[]{:S(2)}) copy-start(f32[16,2,32]{2,1,0:T(2,128)} %e0.1) | copy-start | bytes 12292
  3.6 9.3 %collective-permute-start.1 = (f32[2,16,128]{2,1,0:T(8,128)}, f32[2,16,128]{2,1,0:T(8,128)S(1)}, u32[]{:S(2)}, u32[]{:S(2)}) collective-permute-start(f32[2,16,128]{2,1,0:T(8,128)} %shard_map.119), channel_id=1, source_target_pairs={{1,2},{2,1},{3,4},{4,3},{5,6},{6,5},{7,8},{8,7},{9,10},{10,9},{11,... | collective-permute-start | bytes 49160 | tf_op jit(solution)/shard_map/ppermute | solution.py:585
  8.8 4.7 %collective-permute-start = (f32[2,16,128]{2,1,0:T(8,128)}, f32[2,16,128]{2,1,0:T(8,128)S(1)}, u32[]{:S(2)}, u32[]{:S(2)}) collective-permute-start(f32[2,16,128]{2,1,0:T(8,128)} %shard_map.119), channel_id=1, source_target_pairs={{0,1},{1,0},{2,3},{3,2},{4,5},{5,4},{6,7},{7,6},{8,9},{9,8},{10,11... | collective-permute-start | bytes 49160 | tf_op jit(solution)/shard_map/ppermute | solution.py:584
  13.0 9.9 %copy-start.1 = (f32[16,16,256]{2,1,0:T(8,128)S(1)}, f32[16,16,256]{2,1,0:T(8,128)}, u32[]{:S(2)}) copy-start(f32[16,16,256]{2,1,0:T(8,128)} %e3.1) | copy-start | bytes 786436
  13.5 9.4 %copy-start.7 = (f32[16,16]{1,0:T(8,128)S(1)}, f32[16,16]{1,0:T(8,128)}, u32[]{:S(2)}) copy-start(f32[16,16]{1,0:T(8,128)} %mixing.1) | copy-start | bytes 3076
  13.7 11.2 %collective-permute-start.2 = (f32[7,16,128]{2,1,0:T(8,128)S(1)}, f32[7,16,128]{2,1,0:T(8,128)S(1)}, u32[]{:S(2)}, u32[]{:S(2)}) collective-permute-start(f32[7,16,128]{2,1,0:T(8,128)S(1)} %get-tuple-element.42), channel_id=1, source_target_pairs={{0,32},{32,0},{64,96},{96,64},{128,160},{160,128},{192,224},{224,1... | collective-permute-start | bytes 172040 | tf_op jit(solution)/shard_map/ppermute | solution.py:611
  17.8 7.2 %collective-permute-start.3 = (f32[7,16,128]{2,1,0:T(8,128)S(1)}, f32[7,16,128]{2,1,0:T(8,128)S(1)}, u32[]{:S(2)}, u32[]{:S(2)}) collective-permute-start(f32[7,16,128]{2,1,0:T(8,128)S(1)} %get-tuple-element.43), channel_id=1, source_target_pairs={{32,64},{64,32},{96,128},{128,96},{160,192},{192,160},{224,256},{2... | collective-permute-start | bytes 172040 | tf_op jit(solution)/shard_map/ppermute | solution.py:612

commit v4 on v3

--- a/solution.py
+++ b/solution.py
@@ -57,9 +57,9 @@
     return lax.axis_index("ty"), lax.axis_index("tx")
 
 
-def refine_weight(weights, level, fine_col, coarse_col, a, da):
+def refine_weight(weights, level, fine_col, coarse_col, a, da, along):
     step = coarse_col - (fine_col >> 1)
-    odd = iota((1, 8, coarse_col.shape[2]), 1) & 1
+    odd = iota((1, 8, step.shape[2]), along) & 1
     block = jnp.zeros(step.shape, F32)
     for db in (0, 1, 2):
         n = 3 * da + db
@@ -100,43 +100,58 @@
     return jnp.zeros((count, 128), F32)
 
 
+def lane_range(start, count):
+    return iota((1, 8, count), 2) + start
+
+
+def sublane_range(start, groups):
+    return iota((groups, 8, 128), 0) * 8 + iota((groups, 8, 128), 1) + start
+
+
 def matrix_1(weights):
-    group = iota((9, 8, 128), 0)
-    fine = jnp.where(group < 8, group, HALO[1] // 8) * 8 + iota((9, 8, 128), 1)
-    fine, coarse = both_col(fine, 1, FAR), both_col(lane_index(72), 0, NEAR)
+    coarse, fine = both_col(sublane_range(BASE[0], 5), 0, NEAR), both_col(lane_range(0, 128), 1, FAR)
     rows = []
-    for a in (0, 1):
+    for da in (0, 1, 2):
         row = []
-        for da in (0, 1, 2):
-            block = refine_weight(weights, 1, fine, coarse, a, da)
-            row.append(stack([block[:64], zeros(32), block[64:], zeros(24)]))
+        for a in (0, 1):
+            block = refine_weight(weights, 1, fine, coarse, a, da, 2)
+            row.append(stack([zeros(BASE[0]), block, zeros(88 - BASE[0])]))
         rows.append(row)
     return rows
 
 
 def matrix_2(weights):
-    index, coarse = fine_index(128), both_col(lane_index(128), 1, NEAR)
-    rows = [[refine_weight(weights, 2, index, coarse, a, da) for da in (0, 1, 2)] for a in (0, 1)]
-    index, coarse = HALO[2] + iota((1, 8, 128), 1), coarse[:1]
-    halos = [halo_col(index, 2, HALO[2] + 4 * a, FAR) for a in (0, 1)]
+    group = iota((9, 8, 128), 0)
+    coarse = jnp.where(group < 8, group, HALO[1] // 8) * 8 + iota((9, 8, 128), 1)
+    coarse, lane = both_col(coarse, 1, NEAR), lane_range(0, 128)
+    halos = [halo_col(lane, 2, HALO[2] + 4 * a, FAR) for a in (0, 1)]
+    rows = []
+    for da in (0, 1, 2):
+        row = [refine_weight(weights, 2, lane, coarse, a, da, 2) for a in (0, 1)]
+        row.append(sum(refine_weight(weights, 2, halos[a], coarse, a, da, 2) for a in (0, 1)))
+        rows.append([stack([x[:64], zeros(32), x[64:], zeros(24)]) for x in row])
+    return rows
+
+
+def matrix_3(weights):
+    index = sublane_range(0, 16)
+    halo = sublane_range(HALO[2], 2)
+    rows = []
+    for da in (0, 1, 2):
+        rows.append(
+            [refine_weight(weights, 3, lane_range(128 * h, 128), index, a, da, 2) for a in (0, 1) for h in (0, 1)]
+        )
     row = []
-    for da in (0, 1, 2):
-        block = sum(refine_weight(weights, 2, halos[a], coarse, a, da) for a in (0, 1))
-        row.append(stack([zeros(HALO[2]), block, zeros(120 - HALO[2])]))
+    for a in (0, 1):
+        for h in (0, 1):
+            block = sum(
+                refine_weight(
+                    weights, 3, lane_range(128 * h, 128), halo_col(halo, 2, HALO[2] + 4 * da, NEAR), a, da, 2
+                )
+                for da in (0, 1, 2)
+            )
+            row.append(stack([zeros(HALO[2]), block, zeros(112 - HALO[2])]))
     rows.append(row)
-    return rows
-
-
-def matrix_3(weights):
-    index, lane = fine_index(256), lane_index(256)
-    ends = iota((2, 8, 128), 0) * 248 + iota((2, 8, 128), 1)
-    halos = [halo_col(lane_index(16), 2, HALO[2] + 4 * da, NEAR) for da in (0, 1, 2)]
-    rows = []
-    for a in (0, 1):
-        row = [refine_weight(weights, 3, index, lane, a, da) for da in (0, 1, 2)]
-        block = sum(refine_weight(weights, 3, ends, halos[da], a, da) for da in (0, 1, 2))
-        row.append(stack([block[:8], zeros(240), block[8:]]))
-        rows.append(row)
     return rows
 
 
@@ -222,7 +237,7 @@
         values = []
         for a in (0, 1):
             for b in (0, 1):
-                here, there = 2 * a + b, 2 * (a ^ flip_row) + (b ^ flip_col)
+                here, there = 2 * (a ^ flip_row) + b, 2 * a + (b ^ flip_col)
                 values.append(factor[2, there, here] if transposed else factor[2, here, there])
         return jnp.where(
             odd_row == 0,
@@ -233,8 +248,7 @@
     return (
         coefficient(0, 0) * x
         + coefficient(0, 1) * side
-        + coefficient(1, 0) * swap_rows(x)
-        + coefficient(1, 1) * swap_rows(side)
+        + swap_rows(coefficient(1, 0) * x + coefficient(1, 1) * side)
     )
 
 
@@ -277,7 +291,7 @@
     fine = edge_col(fine_index(width), level, FAR)
     coarse = edge_col(lane_index(width), level - 1, NEAR)
     return split(
-        stack([beside([refine_weight(weights, level, fine, coarse, a, da) for da in (0, 1, 2)]) for a in (0, 1)])
+        stack([beside([refine_weight(weights, level, fine, coarse, a, da, 1) for da in (0, 1, 2)]) for a in (0, 1)])
     )
 
 
@@ -298,14 +312,17 @@
         copies = [
             pltpu.make_async_copy(source, target, sems.at[k])
             for k, (source, target) in enumerate(
-                ((cot_in, cot), (weights_in, weights), (factor_in, factor), (e0_in, e0), (e1_in, e1), (e2_in, e2))
+                ((weights_in, weights), (factor_in, factor), (e0_in, e0), (e1_in, e1), (e2_in, e2))
             )
         ]
+        for q in range(4):
+            part = pl.ds(4 * q, 4)
+            copies.append(pltpu.make_async_copy(cot_in.at[part], cot.at[part], sems.at[5 + q]))
         for copy in copies:
             copy.start()
         ty, tx = places()
         lane = iota((CH, 128), 1)
-        for copy in copies[1:]:
+        for copy in copies[:5]:
             copy.wait()
         edges = [edge_matrix(weights, level, (0, 8, 16, 32)[level]) for level in (1, 2, 3)]
 
@@ -315,7 +332,8 @@
         pieces = [ends(widen(e0[:, r, :]), 0) for r in range(2)]
         pieces += factor_rows([ends(widen(e1[:, r, :]), 1) for r in range(4)], factor, 1, False)
         pieces += factor_rows([ends(e2[:, r, :], 2) for r in range(8)], factor, 2, False)
-        copies[0].wait()
+        for copy in copies[5:]:
+            copy.wait()
         low = cot[:, :, :128].reshape(256, 128)
         high = cot[:, :, 128:].reshape(256, 128)
         edge[...] = jnp.where(iota((256, 128), 1) < 16, low, roll(high, 32))
@@ -337,9 +355,45 @@
     return body
 
 
+def one_hot(test):
+    return jnp.where(test, 1.0, 0.0).astype(BF16)
+
+
+def spread_factor(mixing):
+    parts = split(mixing[...])
+    column = one_hot(iota((256, CH), 0) // CH == iota((256, CH), 1))
+    return parts, column, [dot(column, f, NN).astype(BF16) for f in parts]
+
+
+def select(where, pairs):
+    return [jnp.where(where, dot(x, y, NT), 0.0).astype(BF16) for x, y in pairs]
+
+
+def side_matrices(mixing, side_h, side_l, back_h, back_l):
+    _, column, spread = spread_factor(mixing)
+    same = (iota((256, 256), 0) & 15) == (iota((256, 256), 1) & 15)
+    side_h[...], side_l[...] = select(same, [(f, column) for f in spread])
+    back_h[...], back_l[...] = select(same, [(column, f) for f in spread])
+
+
+def last_matrices(mixing, mix_h, mix_l, back0, back1, back2):
+    parts, _, spread = spread_factor(mixing)
+    tiled = one_hot((iota((256, CH), 0) & 15) == iota((256, CH), 1))
+    col = iota((256, 256), 1)
+    there = (iota((256, 256), 0) & 15) == 2 * ((col & 127) >> 4) + (col >> 7)
+    mix_h[...], mix_l[...] = select(there, [(f, tiled) for f in spread])
+    for ref, rows in ((back0, 2), (back1, 4), (back2, 8)):
+        n = CH * rows
+        one = one_hot(iota((n, CH), 0) // rows == iota((n, CH), 1))
+        full = [dot(one, stack([f] * rows), NT) for f in parts]
+        ref[...] = jnp.where(iota((n, n), 0) % rows == iota((n, n), 1) // CH, full[0] + full[1], 0.0)
+
+
 def inner_kernel(grid):
-    def body(weights, factor, cot, e0, e1, e2, g0, g1, g2, u0, u1, u2, h1, l1, h2, l2, h3, l3, halves):
+    def body(weights, factor, mixing, cot, e0, e1, e2, g0, g1, g2, u0, u1, u2, h1, l1, h2, l2, h3, l3, *rest):
+        *mixes, halves = rest
         ty, tx = places()
+        side_matrices(mixing, *mixes)
         store_matrix(matrix_3(weights), h3, l3)
         store_matrix(matrix_2(weights), h2, l2)
         store_matrix(matrix_1(weights), h1, l1)
@@ -358,7 +412,7 @@
                 for j in (0, 1)
             ]
         )
-        out = mul3(split(left), (h3[...], l3[...]), NN)
+        out = mul3(split(left), (h3[...], l3[...]), NT)
         up2 = block_sum(out, 8, tile)
         side2 = block_sum(tile(out, 3), 8, lambda x, da: roll(x, -4 * da))
         top = inside_mask(HALO[2], tx, grid[1] - 1, False)
@@ -372,12 +426,12 @@
         left = beside(
             [stack(up2[0::2]), stack(up2[1::2]), stack(side2[0::2]) + roll(stack(side2[1::2]), 4)]
         )
-        up1 = block_sum(mul3(split(left), (h2[...], l2[...]), NN), 6, tile)
+        up1 = block_sum(mul3(split(left), (h2[...], l2[...]), NT), 6, tile)
         up1 = clear_outside(up1, 2, inside_mask(HALO[1], tx, grid[1] - 1, True), ty, grid[0] - 1)
         for r, row in enumerate(up1):
             u1[r] = row
         left = beside([stack(up1[0::2]), stack(up1[1::2])])
-        up0 = block_sum(mul3(split(left), (h1[...], l1[...]), NN), 4, tile)
+        up0 = block_sum(mul3(split(left), (h1[...], l1[...]), NT), 4, tile)
         for r, row in enumerate(up0):
             u0[r] = row
 
@@ -446,7 +500,7 @@
 
 
 def third_kernel(grid):
-    def body(factor, got_a, got_b, x0, x1, g2, s2, v0, v1, v2, local, h1, l1, h2, l2, h3, l3, mix_h, mix_l, back0, back1, back2, sky, d0, d1, d2):
+    def body(factor, got_a, got_b, x0, x1, g2, s2, v0, v1, v2, local, grad, h1, l1, h2, l2, h3, l3, mix_h, mix_l, back0, back1, back2, sky, d0, d1, d2, d3):
         ty, tx = places()
         even = (ty & 1) == 0
         above, below = [], []
@@ -459,13 +513,13 @@
             return beside([stack(rows[da : da + len(rows) - 2]) for da in (0, 1, 2)])
 
         field = above[2:4] + [x0[r] for r in range(2)] + below[2:4]
-        out = mul3(split(trio(field)), (h1[...], l1[...]), NT)
+        out = mul3(split(trio(field)), (h1[...], l1[...]), NN)
         mixed = above[2:4] + [x1[r] for r in range(4)] + below[2:4]
         field = [tile(out[CH * i : CH * (i + 1)], a) for i in range(4) for a in (0, 1)]
         field = [f + m for f, m in zip(field, mixed)]
         mask = inside_mask(HALO[1], tx, grid[1] - 1, True)
         field = clear_outside(field, 2, mask, ty, grid[0] - 1)
-        out = mul3(split(trio(field)), (h2[...], l2[...]), NT)
+        out = mul3(split(trio(field)), (h2[...], l2[...]), NN)
         mixed = above[0:2] + [g2[r] for r in range(8)] + below[0:2]
         side = above[2:4] + [s2[r] for r in range(8)] + below[2:4]
         pairs = [(out[CH * i : CH * (i + 1)], a) for i in range(6) for a in (0, 1)]
@@ -475,7 +529,7 @@
         mask = inside_mask(HALO[2], tx, grid[1] - 1, False)
         side = clear_outside(side, 2, mask, ty, grid[0] - 1)[1:11]
         sides = [side[i] + roll(side[i + 1], 4) + roll(side[i + 2], 8) for i in range(8)]
-        out = mul3(split(beside([trio(field), stack(sides)])), (h3[...], l3[...]), NT)
+        out = mul3(split(beside([trio(field), stack(sides)])), (h3[...], l3[...]), NN)
         fine = split(stack([out[:, :256], out[:, 256:]]))
         sky[...] = (mul3((mix_h[...], mix_l[...]), fine, NN) + local[...]).reshape(CH, 16, 256)
 
@@ -491,22 +545,13 @@
                 out = roll(out, -BASE[level])
             out = out.reshape(CH, ROWS[level], 128)
             ref[...] = out[:, :, :cols] if cols < 128 else out
+        d3[...] = grad[...]
 
     return body
 
 
-def one_hot(test):
-    return jnp.where(test, 1.0, 0.0).astype(BF16)
-
-
-def local_body(factor, mixing, cot, e3, local, grad_out, mix_h, mix_l, back0, back1, back2, grad, sem):
-    parts = split(mixing[...])
-    column = one_hot(iota((256, CH), 0) // CH == iota((256, CH), 1))
-    spread = [dot(column, f, NN).astype(BF16) for f in parts]
-    same = (iota((256, 256), 0) & 15) == (iota((256, 256), 1) & 15)
-
-    def select(where, pairs):
-        return [jnp.where(where, dot(x, y, NT), 0.0).astype(BF16) for x, y in pairs]
+def local_body(factor, mixing, cot, e3, side_h, side_l, back_h, back_l, local, grad, *mixes):
+    last_matrices(mixing, *mixes)
 
     def factored(ref, transposed):
         halves = [
@@ -515,22 +560,8 @@
         ]
         return split(beside(halves))
 
-    side = select(same, [(column, f) for f in spread])
-    grad[...] = mul3(side, factored(cot, True), NN).reshape(CH, 16, 256)
-    copy = pltpu.make_async_copy(grad, grad_out, sem)
-    copy.start()
-    side = select(same, [(f, column) for f in spread])
-    local[...] = mul3(side, factored(e3, False), NN)
-    tiled = one_hot((iota((256, CH), 0) & 15) == iota((256, CH), 1))
-    col = iota((256, 256), 1)
-    there = (iota((256, 256), 0) & 15) == 2 * ((col & 127) >> 4) + (col >> 7)
-    mix_h[...], mix_l[...] = select(there, [(f, tiled) for f in spread])
-    for ref, rows in ((back0, 2), (back1, 4), (back2, 8)):
-        n = CH * rows
-        one = one_hot(iota((n, CH), 0) // rows == iota((n, CH), 1))
-        full = [dot(one, stack([f] * rows), NT) for f in parts]
-        ref[...] = jnp.where(iota((n, n), 0) % rows == iota((n, n), 1) // CH, full[0] + full[1], 0.0)
-    copy.wait()
+    grad[...] = mul3((back_h[...], back_l[...]), factored(cot, True), NN).reshape(CH, 16, 256)
+    local[...] = mul3((side_h[...], side_l[...]), factored(e3, False), NN)
 
 
 def swaps(count, first):
@@ -577,45 +608,46 @@
                 pltpu.VMEM((CH, 4, 64), F32),
                 pltpu.VMEM((CH, 8, 128), F32),
                 pltpu.VMEM((256, 128), F32),
-                pltpu.SemaphoreType.DMA((6,)),
+                pltpu.SemaphoreType.DMA((9,)),
             ],
             60 * 1024 * 1024,
         )
         got_a = lax.ppermute(send, "tx", swaps(grid[1], 0))
         got_b = lax.ppermute(send, "tx", swaps(grid[1], 1))
-        sizes = [(256, 384), (384, 384), (512, 512)]
+        sizes = [(384, 256), (384, 384), (512, 512)]
         inner = call(
             inner_kernel(grid),
-            [SMEM] * 2 + [VMEM] * 4,
-            rows + ups + [shaped(*size, dtype=BF16) for size in sizes for _ in (0, 1)],
-            (weights, factor, cot, e0, e1, e2),
+            [SMEM] * 2 + [VMEM] * 5,
+            rows
+            + ups
+            + [shaped(*size, dtype=BF16) for size in sizes for _ in (0, 1)]
+            + [shaped(256, 256, dtype=BF16)] * 4,
+            (weights, factor, mixing, cot, e0, e1, e2),
             [pltpu.VMEM((2, 256, 128), F32)],
         )
-        matrices = inner[6:]
+        matrices, sides = inner[6:12], inner[12:]
         second = call(
             second_kernel(grid),
             [VMEM] * 8,
             [shaped(7, CH, 128)] * 2 + rows + rows,
             (got_a, got_b, *inner[:6]),
         )
-        local, grad3, *mixes = call(
+        local, grad, *mixes = call(
             local_body,
-            [SMEM] + [VMEM] * 3,
+            [SMEM] + [VMEM] * 7,
             [shaped(256, 256), shaped(CH, 16, 256)]
             + [shaped(256, 256, dtype=BF16)] * 2
             + [shaped(32, 32), shaped(64, 64), shaped(128, 128)],
-            (factor, mixing, cot, e3),
-            [pltpu.VMEM((CH, 16, 256), F32), pltpu.SemaphoreType.DMA],
-            into=1,
+            (factor, mixing, cot, e3, *sides),
         )
         got_a = lax.ppermute(second[0], "ty", swaps(grid[0], 0))
         got_b = lax.ppermute(second[1], "ty", swaps(grid[0], 1))
         x0, x1, s2, v0, v1, v2 = second[2:]
-        sky, grad0, grad1, grad2 = call(
+        sky, grad0, grad1, grad2, grad3 = call(
             third_kernel(grid),
-            [SMEM] + [VMEM] * 21,
-            [shaped(CH, 16, 256), shaped(CH, 2, 32), shaped(CH, 4, 64), shaped(CH, 8, 128)],
-            (factor, got_a, got_b, x0, x1, inner[2], s2, v0, v1, v2, local, *matrices, *mixes),
+            [SMEM] + [VMEM] * 22,
+            [shaped(CH, 16, 256), shaped(CH, 2, 32), shaped(CH, 4, 64), shaped(CH, 8, 128), shaped(CH, 16, 256)],
+            (factor, got_a, got_b, x0, x1, inner[2], s2, v0, v1, v2, local, grad, *matrices, *mixes),
         )
         return (sky, grad0, grad1, grad2, grad3)
 

time: 28.4 us -> 28.1 us (0.989)
    ppermute x1, waiting for transfers between devices: 0.54 us -> 0.03 us  [on_device(): got_a = lax.ppermute(send, 'tx', swaps(grid[1], 0))]
    ppermute x1, waiting for transfers between devices: 0.01 us -> 0.43 us  [on_device(): got_b = lax.ppermute(second[1], 'ty', swaps(grid[0], 1))]
  transfers between devices with their start and end apart: 4 -> 4, of which waited for: 1 -> 1; matrix products, arithmetic and copies ran while one was open for 0% -> 0% of each run, Pallas kernels for 15% -> 14%
where the time goes in v4:
time: 28.1 us; the launch traced here: 27.9 us
  starting transfers between devices  16.2 us (58%)
  Pallas kernels  10.4 us (37%)
  between operations  0.84 us (3%)
  waiting for transfers between devices  0.47 us (2%)
    pallas_call x5, Pallas kernels, call(): pl.pallas_call(body, out_shape=outs, in_specs=specs, out_specs=[HBM if k...  10.4 us
    ppermute x1, starting transfers between devices, on_device(): got_b = lax.ppermute(send, 'tx', swaps(grid[1], 1))  5.16 us
    ppermute x1, starting transfers between devices, on_device(): got_b = lax.ppermute(second[1], 'ty', swaps(grid[0], 1))  5.12 us
    ppermute x1, starting transfers between devices, on_device(): got_a = lax.ppermute(second[0], 'ty', swaps(grid[0], 0))  4.01 us
    ppermute x1, starting transfers between devices, on_device(): got_a = lax.ppermute(send, 'tx', swaps(grid[1], 0))  1.92 us
  transfers between devices with their start and end apart: 4, of which 1 were waited for; matrix products, arithmetic and copies ran while one was open for 0% of the time, Pallas kernels for 14%

profile of v4, /device:TPU:249, one launch (start us, length us, event | category | flops | bytes accessed | tf_op | source)
XLA Modules:
  0.0 27.9 jit_solution(5281842306307808049)
XLA Ops:
  0.6 0.0 copy-start.4
  0.6 0.0 copy-start
  0.7 0.0 copy-start.7
  0.7 0.0 copy-start.1
  0.7 0.0 copy-start.3
  0.7 0.0 copy-start.5
  0.7 0.0 copy-start.6
  0.7 3.0 %shard_map.119 = f32[2,16,128]{2,1,0:T(8,128)} custom-call(f32[3,4,9]{2,1,0:T(4,128)} %weights.1, f32[3,4,4]{2,1,0:T(4,128)} %factor.5, f32[16,16,256]{2,1,0:T(8,128)} %cot.3, f32[16,2,32]{2,1,0:T(2,128)} %e0.1, f32[16,4,64]{2,1,0:T(4,128)} %e1.1, f32[16,8,128]{2,1,0:T(8,128)} %e2.1), custom_call_target="tpu_custom_call" | custom-call | tf_op jit(solution)/shard_map/pallas_call | solution.py:584
  3.7 5.2 %collective-permute-start.1 = (f32[2,16,128]{2,1,0:T(8,128)}, f32[2,16,128]{2,1,0:T(8,128)S(1)}, u32[]{:S(2)}, u32[]{:S(2)}) collective-permute-start(f32[2,16,128]{2,1,0:T(8,128)} %shard_map.119), channel_id=1, source_target_pairs={{1,2},{2,1},{3,4},{4,3},{5,6},{6,5},{7,8},{8,7},{9,10},{10,9},{11,... | collective-permute-start | bytes 49160 | tf_op jit(solution)/shard_map/ppermute | solution.py:616
  8.9 1.9 %collective-permute-start = (f32[2,16,128]{2,1,0:T(8,128)}, f32[2,16,128]{2,1,0:T(8,128)S(1)}, u32[]{:S(2)}, u32[]{:S(2)}) collective-permute-start(f32[2,16,128]{2,1,0:T(8,128)} %shard_map.119), channel_id=1, source_target_pairs={{0,1},{1,0},{2,3},{3,2},{4,5},{5,4},{6,7},{7,6},{8,9},{9,8},{10,11... | collective-permute-start | bytes 49160 | tf_op jit(solution)/shard_map/ppermute | solution.py:615
  10.8 0.0 copy-done.4
  10.8 0.0 copy-done
  10.8 0.0 copy-done.7
  10.8 0.0 copy-done.1
  10.8 0.0 copy-done.3
  10.8 0.0 copy-done.5
  10.9 0.0 copy-done.6
  10.9 2.6 %shard_map.120 = (f32[2,16,128]{2,1,0:T(8,128)S(1)}, f32[4,16,128]{2,1,0:T(8,128)S(1)}, f32[8,16,128]{2,1,0:T(8,128)S(1)}, f32[6,16,128]{2,1,0:T(8,128)S(1)}, f3...) custom-call(f32[3,4,9]{2,1,0:T(4,128)S(1)} %copy-done.7, ...), custom_call_target="tpu_custom_call" | custom-call | tf_op jit(solution)/shard_map/pallas_call | solution.py:584
  13.5 0.0 copy-start.2
  13.5 0.0 collective-permute-done.1.got_b
  13.5 0.0 collective-permute-done.got_a
  13.6 0.2 shard_map.121
  13.8 4.0 %collective-permute-start.2 = (f32[7,16,128]{2,1,0:T(8,128)S(1)}, f32[7,16,128]{2,1,0:T(8,128)S(1)}, u32[]{:S(2)}, u32[]{:S(2)}) collective-permute-start(f32[7,16,128]{2,1,0:T(8,128)S(1)} %get-tuple-element.42), channel_id=1, source_target_pairs={{0,32},{32,0},{64,96},{96,64},{128,160},{160,128},{192,224},{224,1... | collective-permute-start | bytes 172040 | tf_op jit(solution)/shard_map/ppermute | solution.py:643
  17.8 5.1 %collective-permute-start.3 = (f32[7,16,128]{2,1,0:T(8,128)S(1)}, f32[7,16,128]{2,1,0:T(8,128)S(1)}, u32[]{:S(2)}, u32[]{:S(2)}) collective-permute-start(f32[7,16,128]{2,1,0:T(8,128)S(1)} %get-tuple-element.43), channel_id=1, source_target_pairs={{32,64},{64,32},{96,128},{128,96},{160,192},{192,160},{224,256},{2... | collective-permute-start | bytes 172040 | tf_op jit(solution)/shard_map/ppermute | solution.py:644
  22.9 0.0 copy-done.2
  22.9 1.4 %shard_map.122 = (f32[256,256]{1,0:T(8,128)S(1)}, f32[16,16,256]{2,1,0:T(8,128)S(1)}, bf16[256,256]{1,0:T(8,128)(2,1)S(1)}, bf16[256,256]{1,0:T(8,128)(2,1)S(1)}...) custom-call(f32[3,4,4]{2,1,0:T(4,128)S(1)} %copy-done.4, f32[16,16]{1,0:T(8,128)S(1)} %copy-done.6, ...), custom_call_target="tpu_custom_call" | custom-call | tf_op jit(solution)/shard_map/pallas_call | solution.py:584
  24.3 0.0 collective-permute-done.2.got_a
  24.3 0.4 %collective-permute-done.3.got_b = f32[7,16,128]{2,1,0:T(8,128)S(1)} collective-permute-done((f32[7,16,128]{2,1,0:T(8,128)S(1)}, f32[7,16,128]{2,1,0:T(8,128)S(1)}, u32[]{:S(2)}, u32[]{:S(2)}) %collective-permute-start.3) | collective-permute-done | bytes 57376 | tf_op jit(solution)/shard_map/ppermute | solution.py:644
  24.8 3.1 %shard_map.123 = (f32[16,16,256]{2,1,0:T(8,128)}, f32[16,2,32]{2,1,0:T(2,128)}, f32[16,4,64]{2,1,0:T(4,128)}, f32[16,8,128]{2,1,0:T(8,128)}, f32[16,16,256]{2,1,0:T(8,128)}) custom-call(f32[3,4,4]{2,1,0:T(4,128)S(1)} %copy-done.4, f32[7,16,128]{2,1,0:T(8,128)S(1)} %collective-permute-done.2.got_a, f32[7,16,128]{2,1,0:T(8,128)S(1)} %collective-permute-done.3.got_b, ...), custom_call_target="tpu_custom_call" | custom-call | tf_op jit(solution)/shard_map/pallas_call | solution.py:584
Async XLA Ops:
  0.6 10.2 %copy-start.4 = (f32[3,4,4]{2,1,0:T(4,128)S(1)}, f32[3,4,4]{2,1,0:T(4,128)}, u32[]{:S(2)}) copy-start(f32[3,4,4]{2,1,0:T(4,128)} %factor.5) | copy-start | bytes 580
  0.6 10.2 %copy-start = (f32[16,16,256]{2,1,0:T(8,128)S(1)}, f32[16,16,256]{2,1,0:T(8,128)}, u32[]{:S(2)}) copy-start(f32[16,16,256]{2,1,0:T(8,128)} %cot.3) | copy-start | bytes 786436
  0.7 10.2 %copy-start.7 = (f32[3,4,9]{2,1,0:T(4,128)S(1)}, f32[3,4,9]{2,1,0:T(4,128)}, u32[]{:S(2)}) copy-start(f32[3,4,9]{2,1,0:T(4,128)} %weights.1) | copy-start | bytes 1300
  0.7 10.2 %copy-start.1 = (f32[16,8,128]{2,1,0:T(8,128)S(1)}, f32[16,8,128]{2,1,0:T(8,128)}, u32[]{:S(2)}) copy-start(f32[16,8,128]{2,1,0:T(8,128)} %e2.1) | copy-start | bytes 196612
  0.7 10.2 %copy-start.3 = (f32[16,4,64]{2,1,0:T(4,128)S(1)}, f32[16,4,64]{2,1,0:T(4,128)}, u32[]{:S(2)}) copy-start(f32[16,4,64]{2,1,0:T(4,128)} %e1.1) | copy-start | bytes 49156
  0.7 10.2 %copy-start.5 = (f32[16,2,32]{2,1,0:T(2,128)S(1)}, f32[16,2,32]{2,1,0:T(2,128)}, u32[]{:S(2)}) copy-start(f32[16,2,32]{2,1,0:T(2,128)} %e0.1) | copy-start | bytes 12292
  0.7 10.2 %copy-start.6 = (f32[16,16]{1,0:T(8,128)S(1)}, f32[16,16]{1,0:T(8,128)}, u32[]{:S(2)}) copy-start(f32[16,16]{1,0:T(8,128)} %mixing.3) | copy-start | bytes 3076
  3.7 9.8 %collective-permute-start.1 = (f32[2,16,128]{2,1,0:T(8,128)}, f32[2,16,128]{2,1,0:T(8,128)S(1)}, u32[]{:S(2)}, u32[]{:S(2)}) collective-permute-start(f32[2,16,128]{2,1,0:T(8,128)} %shard_map.119), channel_id=1, source_target_pairs={{1,2},{2,1},{3,4},{4,3},{5,6},{6,5},{7,8},{8,7},{9,10},{10,9},{11,... | collective-permute-start | bytes 49160 | tf_op jit(solution)/shard_map/ppermute | solution.py:616
  8.9 4.7 %collective-permute-start = (f32[2,16,128]{2,1,0:T(8,128)}, f32[2,16,128]{2,1,0:T(8,128)S(1)}, u32[]{:S(2)}, u32[]{:S(2)}) collective-permute-start(f32[2,16,128]{2,1,0:T(8,128)} %shard_map.119), channel_id=1, source_target_pairs={{0,1},{1,0},{2,3},{3,2},{4,5},{5,4},{6,7},{7,6},{8,9},{9,8},{10,11... | collective-permute-start | bytes 49160 | tf_op jit(solution)/shard_map/ppermute | solution.py:615
  13.5 9.4 %copy-start.2 = (f32[16,16,256]{2,1,0:T(8,128)S(1)}, f32[16,16,256]{2,1,0:T(8,128)}, u32[]{:S(2)}) copy-start(f32[16,16,256]{2,1,0:T(8,128)} %e3.1) | copy-start | bytes 786436
  13.8 10.6 %collective-permute-start.2 = (f32[7,16,128]{2,1,0:T(8,128)S(1)}, f32[7,16,128]{2,1,0:T(8,128)S(1)}, u32[]{:S(2)}, u32[]{:S(2)}) collective-permute-start(f32[7,16,128]{2,1,0:T(8,128)S(1)} %get-tuple-element.42), channel_id=1, source_target_pairs={{0,32},{32,0},{64,96},{96,64},{128,160},{160,128},{192,224},{224,1... | collective-permute-start | bytes 172040 | tf_op jit(solution)/shard_map/ppermute | solution.py:643
  17.8 7.0 %collective-permute-start.3 = (f32[7,16,128]{2,1,0:T(8,128)S(1)}, f32[7,16,128]{2,1,0:T(8,128)S(1)}, u32[]{:S(2)}, u32[]{:S(2)}) collective-permute-start(f32[7,16,128]{2,1,0:T(8,128)S(1)} %get-tuple-element.43), channel_id=1, source_target_pairs={{32,64},{64,32},{96,128},{128,96},{160,192},{192,160},{224,256},{2... | collective-permute-start | bytes 172040 | tf_op jit(solution)/shard_map/ppermute | solution.py:644

commit v5 on v4

--- a/solution.py
+++ b/solution.py
@@ -325,6 +325,8 @@
         for copy in copies[:5]:
             copy.wait()
         edges = [edge_matrix(weights, level, (0, 8, 16, 32)[level]) for level in (1, 2, 3)]
+        for copy in copies[5:]:
+            copy.wait()
 
         def ends(row, level):
             return jnp.where(lane < 2, row, roll(row, 4 - COLS[level]))
@@ -332,8 +334,6 @@
         pieces = [ends(widen(e0[:, r, :]), 0) for r in range(2)]
         pieces += factor_rows([ends(widen(e1[:, r, :]), 1) for r in range(4)], factor, 1, False)
         pieces += factor_rows([ends(e2[:, r, :], 2) for r in range(8)], factor, 2, False)
-        for copy in copies[5:]:
-            copy.wait()
         low = cot[:, :, :128].reshape(256, 128)
         high = cot[:, :, 128:].reshape(256, 128)
         edge[...] = jnp.where(iota((256, 128), 1) < 16, low, roll(high, 32))

time: 28.1 us -> 28 us (level)
  no operation moved by 1% of the time
where the time goes in v5:
time: 28 us; the launch traced here: 27.8 us
  starting transfers between devices  16.2 us (58%)
  Pallas kernels  10.2 us (36%)
  between operations  0.84 us (3%)
  waiting for transfers between devices  0.47 us (2%)
    pallas_call x5, Pallas kernels, call(): pl.pallas_call(body, out_shape=outs, in_specs=specs, out_specs=[HBM if k...  10.2 us
    ppermute x1, starting transfers between devices, on_device(): got_b = lax.ppermute(send, 'tx', swaps(grid[1], 1))  5.17 us
    ppermute x1, starting transfers between devices, on_device(): got_b = lax.ppermute(second[1], 'ty', swaps(grid[0], 1))  5.12 us
    ppermute x1, starting transfers between devices, on_device(): got_a = lax.ppermute(second[0], 'ty', swaps(grid[0], 0))  4.01 us
    ppermute x1, starting transfers between devices, on_device(): got_a = lax.ppermute(send, 'tx', swaps(grid[1], 0))  1.92 us
  transfers between devices with their start and end apart: 4, of which 1 were waited for; matrix products, arithmetic and copies ran while one was open for 0% of the time, Pallas kernels for 14%

profile of v5, /device:TPU:249, one launch (start us, length us, event | category | flops | bytes accessed | tf_op | source)
XLA Modules:
  0.0 27.8 jit_solution(17302838070393339559)
XLA Ops:
  0.6 0.0 copy-start.4
  0.6 0.0 copy-start
  0.7 0.0 copy-start.7
  0.7 0.0 copy-start.1
  0.7 0.0 copy-start.3
  0.7 0.0 copy-start.5
  0.7 0.0 copy-start.6
  0.7 2.8 %shard_map.119 = f32[2,16,128]{2,1,0:T(8,128)} custom-call(f32[3,4,9]{2,1,0:T(4,128)} %weights.1, f32[3,4,4]{2,1,0:T(4,128)} %factor.5, f32[16,16,256]{2,1,0:T(8,128)} %cot.3, f32[16,2,32]{2,1,0:T(2,128)} %e0.1, f32[16,4,64]{2,1,0:T(4,128)} %e1.1, f32[16,8,128]{2,1,0:T(8,128)} %e2.1), custom_call_target="tpu_custom_call" | custom-call | tf_op jit(solution)/shard_map/pallas_call | solution.py:584
  3.5 5.2 %collective-permute-start.1 = (f32[2,16,128]{2,1,0:T(8,128)}, f32[2,16,128]{2,1,0:T(8,128)S(1)}, u32[]{:S(2)}, u32[]{:S(2)}) collective-permute-start(f32[2,16,128]{2,1,0:T(8,128)} %shard_map.119), channel_id=1, source_target_pairs={{1,2},{2,1},{3,4},{4,3},{5,6},{6,5},{7,8},{8,7},{9,10},{10,9},{11,... | collective-permute-start | bytes 49160 | tf_op jit(solution)/shard_map/ppermute | solution.py:616
  8.7 1.9 %collective-permute-start = (f32[2,16,128]{2,1,0:T(8,128)}, f32[2,16,128]{2,1,0:T(8,128)S(1)}, u32[]{:S(2)}, u32[]{:S(2)}) collective-permute-start(f32[2,16,128]{2,1,0:T(8,128)} %shard_map.119), channel_id=1, source_target_pairs={{0,1},{1,0},{2,3},{3,2},{4,5},{5,4},{6,7},{7,6},{8,9},{9,8},{10,11... | collective-permute-start | bytes 49160 | tf_op jit(solution)/shard_map/ppermute | solution.py:615
  10.6 0.0 copy-done.4
  10.6 0.0 copy-done
  10.7 0.0 copy-done.7
  10.7 0.0 copy-done.1
  10.7 0.0 copy-done.3
  10.7 0.0 copy-done.5
  10.7 0.0 copy-done.6
  10.7 2.6 %shard_map.120 = (f32[2,16,128]{2,1,0:T(8,128)S(1)}, f32[4,16,128]{2,1,0:T(8,128)S(1)}, f32[8,16,128]{2,1,0:T(8,128)S(1)}, f32[6,16,128]{2,1,0:T(8,128)S(1)}, f3...) custom-call(f32[3,4,9]{2,1,0:T(4,128)S(1)} %copy-done.7, ...), custom_call_target="tpu_custom_call" | custom-call | tf_op jit(solution)/shard_map/pallas_call | solution.py:584
  13.3 0.0 copy-start.2
  13.4 0.0 collective-permute-done.1.got_b
  13.4 0.0 collective-permute-done.got_a
  13.4 0.2 shard_map.121
  13.6 4.0 %collective-permute-start.2 = (f32[7,16,128]{2,1,0:T(8,128)S(1)}, f32[7,16,128]{2,1,0:T(8,128)S(1)}, u32[]{:S(2)}, u32[]{:S(2)}) collective-permute-start(f32[7,16,128]{2,1,0:T(8,128)S(1)} %get-tuple-element.42), channel_id=1, source_target_pairs={{0,32},{32,0},{64,96},{96,64},{128,160},{160,128},{192,224},{224,1... | collective-permute-start | bytes 172040 | tf_op jit(solution)/shard_map/ppermute | solution.py:643
  17.6 5.1 %collective-permute-start.3 = (f32[7,16,128]{2,1,0:T(8,128)S(1)}, f32[7,16,128]{2,1,0:T(8,128)S(1)}, u32[]{:S(2)}, u32[]{:S(2)}) collective-permute-start(f32[7,16,128]{2,1,0:T(8,128)S(1)} %get-tuple-element.43), channel_id=1, source_target_pairs={{32,64},{64,32},{96,128},{128,96},{160,192},{192,160},{224,256},{2... | collective-permute-start | bytes 172040 | tf_op jit(solution)/shard_map/ppermute | solution.py:644
  22.8 0.0 copy-done.2
  22.8 1.4 %shard_map.122 = (f32[256,256]{1,0:T(8,128)S(1)}, f32[16,16,256]{2,1,0:T(8,128)S(1)}, bf16[256,256]{1,0:T(8,128)(2,1)S(1)}, bf16[256,256]{1,0:T(8,128)(2,1)S(1)}...) custom-call(f32[3,4,4]{2,1,0:T(4,128)S(1)} %copy-done.4, f32[16,16]{1,0:T(8,128)S(1)} %copy-done.6, ...), custom_call_target="tpu_custom_call" | custom-call | tf_op jit(solution)/shard_map/pallas_call | solution.py:584
  24.2 0.0 collective-permute-done.2.got_a
  24.2 0.4 %collective-permute-done.3.got_b = f32[7,16,128]{2,1,0:T(8,128)S(1)} collective-permute-done((f32[7,16,128]{2,1,0:T(8,128)S(1)}, f32[7,16,128]{2,1,0:T(8,128)S(1)}, u32[]{:S(2)}, u32[]{:S(2)}) %collective-permute-start.3) | collective-permute-done | bytes 57376 | tf_op jit(solution)/shard_map/ppermute | solution.py:644
  24.6 3.1 %shard_map.123 = (f32[16,16,256]{2,1,0:T(8,128)}, f32[16,2,32]{2,1,0:T(2,128)}, f32[16,4,64]{2,1,0:T(4,128)}, f32[16,8,128]{2,1,0:T(8,128)}, f32[16,16,256]{2,1,0:T(8,128)}) custom-call(f32[3,4,4]{2,1,0:T(4,128)S(1)} %copy-done.4, f32[7,16,128]{2,1,0:T(8,128)S(1)} %collective-permute-done.2.got_a, f32[7,16,128]{2,1,0:T(8,128)S(1)} %collective-permute-done.3.got_b, ...), custom_call_target="tpu_custom_call" | custom-call | tf_op jit(solution)/shard_map/pallas_call | solution.py:584
Async XLA Ops:
  0.6 10.0 %copy-start.4 = (f32[3,4,4]{2,1,0:T(4,128)S(1)}, f32[3,4,4]{2,1,0:T(4,128)}, u32[]{:S(2)}) copy-start(f32[3,4,4]{2,1,0:T(4,128)} %factor.5) | copy-start | bytes 580
  0.6 10.0 %copy-start = (f32[16,16,256]{2,1,0:T(8,128)S(1)}, f32[16,16,256]{2,1,0:T(8,128)}, u32[]{:S(2)}) copy-start(f32[16,16,256]{2,1,0:T(8,128)} %cot.3) | copy-start | bytes 786436
  0.7 10.0 %copy-start.7 = (f32[3,4,9]{2,1,0:T(4,128)S(1)}, f32[3,4,9]{2,1,0:T(4,128)}, u32[]{:S(2)}) copy-start(f32[3,4,9]{2,1,0:T(4,128)} %weights.1) | copy-start | bytes 1300
  0.7 10.0 %copy-start.1 = (f32[16,8,128]{2,1,0:T(8,128)S(1)}, f32[16,8,128]{2,1,0:T(8,128)}, u32[]{:S(2)}) copy-start(f32[16,8,128]{2,1,0:T(8,128)} %e2.1) | copy-start | bytes 196612
  0.7 10.0 %copy-start.3 = (f32[16,4,64]{2,1,0:T(4,128)S(1)}, f32[16,4,64]{2,1,0:T(4,128)}, u32[]{:S(2)}) copy-start(f32[16,4,64]{2,1,0:T(4,128)} %e1.1) | copy-start | bytes 49156
  0.7 10.0 %copy-start.5 = (f32[16,2,32]{2,1,0:T(2,128)S(1)}, f32[16,2,32]{2,1,0:T(2,128)}, u32[]{:S(2)}) copy-start(f32[16,2,32]{2,1,0:T(2,128)} %e0.1) | copy-start | bytes 12292
  0.7 10.0 %copy-start.6 = (f32[16,16]{1,0:T(8,128)S(1)}, f32[16,16]{1,0:T(8,128)}, u32[]{:S(2)}) copy-start(f32[16,16]{1,0:T(8,128)} %mixing.3) | copy-start | bytes 3076
  3.5 9.8 %collective-permute-start.1 = (f32[2,16,128]{2,1,0:T(8,128)}, f32[2,16,128]{2,1,0:T(8,128)S(1)}, u32[]{:S(2)}, u32[]{:S(2)}) collective-permute-start(f32[2,16,128]{2,1,0:T(8,128)} %shard_map.119), channel_id=1, source_target_pairs={{1,2},{2,1},{3,4},{4,3},{5,6},{6,5},{7,8},{8,7},{9,10},{10,9},{11,... | collective-permute-start | bytes 49160 | tf_op jit(solution)/shard_map/ppermute | solution.py:616
  8.7 4.7 %collective-permute-start = (f32[2,16,128]{2,1,0:T(8,128)}, f32[2,16,128]{2,1,0:T(8,128)S(1)}, u32[]{:S(2)}, u32[]{:S(2)}) collective-permute-start(f32[2,16,128]{2,1,0:T(8,128)} %shard_map.119), channel_id=1, source_target_pairs={{0,1},{1,0},{2,3},{3,2},{4,5},{5,4},{6,7},{7,6},{8,9},{9,8},{10,11... | collective-permute-start | bytes 49160 | tf_op jit(solution)/shard_map/ppermute | solution.py:615
  13.3 9.4 %copy-start.2 = (f32[16,16,256]{2,1,0:T(8,128)S(1)}, f32[16,16,256]{2,1,0:T(8,128)}, u32[]{:S(2)}) copy-start(f32[16,16,256]{2,1,0:T(8,128)} %e3.1) | copy-start | bytes 786436
  13.6 10.6 %collective-permute-start.2 = (f32[7,16,128]{2,1,0:T(8,128)S(1)}, f32[7,16,128]{2,1,0:T(8,128)S(1)}, u32[]{:S(2)}, u32[]{:S(2)}) collective-permute-start(f32[7,16,128]{2,1,0:T(8,128)S(1)} %get-tuple-element.42), channel_id=1, source_target_pairs={{0,32},{32,0},{64,96},{96,64},{128,160},{160,128},{192,224},{224,1... | collective-permute-start | bytes 172040 | tf_op jit(solution)/shard_map/ppermute | solution.py:643
  17.6 7.0 %collective-permute-start.3 = (f32[7,16,128]{2,1,0:T(8,128)S(1)}, f32[7,16,128]{2,1,0:T(8,128)S(1)}, u32[]{:S(2)}, u32[]{:S(2)}) collective-permute-start(f32[7,16,128]{2,1,0:T(8,128)S(1)} %get-tuple-element.43), channel_id=1, source_target_pairs={{32,64},{64,32},{96,128},{128,96},{160,192},{192,160},{224,256},{2... | collective-permute-start | bytes 172040 | tf_op jit(solution)/shard_map/ppermute | solution.py:644
